TPU v7x, 128 devices: a whole 4x4x4 slice. The times are simulated.
128 devices in a mesh: exp: 32 (over x, y, core), tp: 4 (over z).
Axes of the slice: x: 4, y: 4, z: 4, core: 2. Of those that a mesh axis runs over, the one named last changes fastest.
Arguments:
- audio_feats: bfloat16 [16384, 1280], P(('exp', 'tp')), may hold values from -6 to 6
- w_audio: bfloat16 [1280, 2048], P(None, 'tp'), may hold values from -0.15625 to 0.15625
- b_audio: float32 [2048], replicated, may hold values from -3 to 3
- segments: int32 [32, 512], P('exp'), may hold values from 0 to 3, never falling along the last dimension, each value on 1 to 256 neighbouring positions
- w_q: bfloat16 [2048, 4096], P(None, 'tp'), may hold values from -0.125 to 0.125
- w_k: bfloat16 [2048, 512], P(None, 'tp'), may hold values from -0.125 to 0.125
- w_v: bfloat16 [2048, 512], P(None, 'tp'), may hold values from -0.125 to 0.125
- w_o: bfloat16 [4096, 2048], P('tp'), may hold values from -0.09375 to 0.09375
- attn_gain: float32 [2048], replicated, may hold values from 0.1 to 1.9
- q_gain: float32 [128], replicated, may hold values from 0.5 to 2
- k_gain: float32 [128], replicated, may hold values from 0.5 to 2
- moe_gain: float32 [2048], replicated, may hold values from 0.1 to 1.9
- w_router: bfloat16 [2048, 128], replicated
- routes: int32 [16384, 8], P(('exp', 'tp')), may hold values from 0 to 127, all different within a row; in each aligned block of 128 rows (0 to 127, 128 to 255, ...) at most 16 rows name the same one
- w_gate_up: bfloat16 [128, 2048, 1536], P(('exp', 'tp')), may hold values from -0.125 to 0.125
- w_down: bfloat16 [128, 768, 2048], P(('exp', 'tp')), may hold values from -0.625 to 0.625
Outputs:
- mixed: bfloat16 [16384, 2048], P(('exp', 'tp'))
Inputs may be any that keep to these rules, and one draw needn't show every extreme that they name: `routes`: among the tokens of one device (aligned blocks of 128 rows) no expert id is named more than 16 times, a bound that some block reaches; the ids of one token differ. `segments`: ids never fall along a sequence; each id holds 1 to 256 positions, some exactly that many.
All inputs are finite; a program needn't handle non-finite values.
Results may differ from a plain program's by a relative error of at most 0.02.
Values may be sent and summed in bfloat16 or wider, within the bound.
No kernel may reach another device: no remote copies, remote signals or barrier semaphores. Data moves between devices by JAX's collectives and lax.ppermute only.
A program may use at most 128 MiB of HBM per device.

v0:
```python
import jax
import jax.numpy as jnp
from jax import lax
from jax.sharding import PartitionSpec as P

EPSILON = 1e-06
ROPE_BASE = 1000000.0


def rms_norm(values_in, gain_vec):
    squares = jnp.mean(values_in * values_in, axis=-1, keepdims=True)
    return values_in * lax.rsqrt(squares + EPSILON) * gain_vec


def rope_tables(seq_len, head_dim):
    half_dim = head_dim // 2
    inv_freq = ROPE_BASE ** (-(jnp.arange(half_dim, dtype=jnp.float32) * 2.0) / head_dim)
    angles = jnp.arange(seq_len, dtype=jnp.float32)[:, None] * inv_freq[None, :]
    return (jnp.cos(angles)[:, None, :], jnp.sin(angles)[:, None, :])


def rotate(field, cos_table, sin_table):
    half_dim = field.shape[-1] // 2
    first = field[..., :half_dim]
    second = field[..., half_dim:]
    return jnp.concatenate(
        [first * cos_table - second * sin_table, second * cos_table + first * sin_table], axis=-1
    )


def project_heads(normed, weight, gain_vec, head_dim, cos_table, sin_table):
    raw = jnp.dot(normed, weight, preferred_element_type=jnp.float32)
    raw = raw.reshape(normed.shape[0], weight.shape[1] // head_dim, head_dim)
    return rotate(rms_norm(raw, gain_vec), cos_table, sin_table).astype(jnp.bfloat16)


def local_context(x_seq, seg_ids, w_q, w_k, w_v, attn_gain, q_gain, k_gain):
    seq_len = x_seq.shape[0]
    head_dim = q_gain.shape[0]
    cos_table, sin_table = rope_tables(seq_len, head_dim)
    normed = rms_norm(x_seq.astype(jnp.float32), attn_gain).astype(jnp.bfloat16)
    queries = project_heads(normed, w_q, q_gain, head_dim, cos_table, sin_table)
    keys_rot = project_heads(normed, w_k, k_gain, head_dim, cos_table, sin_table)
    kv_local = keys_rot.shape[1]
    values = (
        jnp.dot(normed, w_v, preferred_element_type=jnp.float32)
        .astype(jnp.bfloat16)
        .reshape(seq_len, kv_local, head_dim)
    )
    group = queries.shape[1] // kv_local
    grouped = queries.reshape(seq_len, kv_local, group, head_dim)
    scores = jnp.einsum(
        "skgd,tkd->kgst", grouped, keys_rot, preferred_element_type=jnp.float32
    ) / jnp.sqrt(jnp.float32(head_dim))
    index = jnp.arange(seq_len)
    allowed = (seg_ids[:, None] == seg_ids[None, :]) & (index[None, :] <= index[:, None])
    scores = jnp.where(allowed, scores, -jnp.inf)
    peak = jnp.max(scores, axis=-1, keepdims=True)
    expo = jnp.exp(scores - peak)
    weights = (expo / jnp.sum(expo, axis=-1, keepdims=True)).astype(jnp.bfloat16)
    context = jnp.einsum("kgst,tkd->skgd", weights, values, preferred_element_type=jnp.float32)
    return context.astype(jnp.bfloat16).reshape(seq_len, queries.shape[1] * head_dim)


def on_device(
    audio_feats,
    w_audio,
    b_audio,
    segments,
    w_q,
    w_k,
    w_v,
    w_o,
    attn_gain,
    q_gain,
    k_gain,
    moe_gain,
    w_router,
    routes,
    w_gate_up,
    w_down,
):
    tp_index = lax.axis_index("tp")
    tok_rows = audio_feats.shape[0]
    feat_dim = b_audio.shape[0]
    seq_audio = lax.all_gather(audio_feats, "tp", axis=0, tiled=True)
    col_width = w_audio.shape[1]
    bias_part = lax.dynamic_slice_in_dim(b_audio, tp_index * col_width, col_width, 0)
    columns = (jnp.dot(seq_audio, w_audio, preferred_element_type=jnp.float32) + bias_part).astype(
        jnp.bfloat16
    )
    x_seq = lax.all_gather(columns, "tp", axis=1, tiled=True)
    x_mine = lax.dynamic_slice_in_dim(x_seq, tp_index * tok_rows, tok_rows, 0)
    context = local_context(x_seq, segments[0], w_q, w_k, w_v, attn_gain, q_gain, k_gain)
    summed = lax.psum(
        jnp.dot(context, w_o, preferred_element_type=jnp.float32).astype(jnp.bfloat16), "tp"
    ).astype(jnp.float32)
    attn_out = lax.dynamic_slice_in_dim(summed, tp_index * tok_rows, tok_rows, 0)
    hidden_res = x_mine.astype(jnp.float32) + attn_out
    normed = rms_norm(hidden_res, moe_gain).astype(jnp.bfloat16)
    logits = jnp.dot(normed, w_router, preferred_element_type=jnp.float32)
    chosen = jnp.take_along_axis(logits, routes, axis=1)
    gates = jax.nn.softmax(chosen, axis=-1).astype(jnp.bfloat16)
    experts = w_router.shape[1]
    top_count = routes.shape[1]
    slot_cap = max(4, 2 * tok_rows * top_count // experts)
    flat_ids = routes.reshape(-1)
    one_hot = (flat_ids[:, None] == jnp.arange(experts, dtype=jnp.int32)[None, :]).astype(jnp.int32)
    earlier = jnp.cumsum(one_hot, axis=0) - one_hot
    position = jnp.sum(earlier * one_hot, axis=1)
    slot_grid = (flat_ids * slot_cap + position).reshape(tok_rows, top_count)
    slot_ids = jnp.arange(experts * slot_cap, dtype=jnp.int32)
    dispatch = jnp.any(slot_grid[None, :, :] == slot_ids[:, None, None], axis=2).astype(
        jnp.bfloat16
    )
    combine = jnp.sum(
        jnp.where(
            slot_grid[:, :, None] == slot_ids[None, None, :],
            gates[:, :, None].astype(jnp.float32),
            jnp.float32(0.0),
        ),
        axis=1,
    ).astype(jnp.bfloat16)
    outgoing = jnp.dot(dispatch, normed, preferred_element_type=jnp.float32).astype(jnp.bfloat16)
    outgoing = outgoing.reshape(experts, slot_cap, feat_dim)
    ff_width = w_down.shape[1]
    slot_block = lax.all_to_all(outgoing, ("exp", "tp"), split_axis=0, concat_axis=0, tiled=True)
    source, slot_count, width_in = slot_block.shape
    flat_rows = slot_block.reshape(source * slot_count, width_in)
    gate_up = jnp.dot(flat_rows, w_gate_up[0], preferred_element_type=jnp.float32)
    hidden = (jax.nn.silu(gate_up[:, :ff_width]) * gate_up[:, ff_width:]).astype(jnp.bfloat16)
    expert_out = jnp.dot(hidden, w_down[0], preferred_element_type=jnp.float32).astype(jnp.bfloat16)
    returned = lax.all_to_all(
        expert_out.reshape(source, slot_count, width_in),
        ("exp", "tp"),
        split_axis=0,
        concat_axis=0,
        tiled=True,
    )
    moe_out = jnp.dot(
        combine, returned.reshape(experts * slot_cap, feat_dim), preferred_element_type=jnp.float32
    )
    return (hidden_res + moe_out).astype(jnp.bfloat16)


def solution(mesh):
    in_specs = (
        P(("exp", "tp"), None),
        P(None, "tp"),
        P(),
        P("exp", None),
        P(None, "tp"),
        P(None, "tp"),
        P(None, "tp"),
        P("tp", None),
        P(),
        P(),
        P(),
        P(),
        P(),
        P(("exp", "tp"), None),
        P(("exp", "tp"), None, None),
        P(("exp", "tp"), None, None),
    )
    out_specs = P(("exp", "tp"), None)
    return jax.shard_map(
        on_device, mesh=mesh, in_specs=in_specs, out_specs=out_specs, check_vma=False
    )
```

profile of v0, /device:TPU:0, one launch (start us, length us, event | category | flops | bytes accessed | tf_op | source)
XLA Modules:
  0.0 437.3 jit_solution(6166757357626474342)
XLA Ops:
  7.3 0.9 dynamic_slice.9
  8.2 28.4 %all-gather.3.cloned.1.call-done = bf16[512,1280]{1,0:T(8,128)(2,1)} async-done(((bf16[128,1280]{1,0:T(8,128)(2,1)}), bf16[512,1280]{1,0:T(8,128)(2,1)}) %all-gather.3.cloned.1.call-update) | async-done | bytes 1310736 | tf_op jit(solution)/shard_map/all_gather | solution.py:86
  36.7 3.3 fusion.20
  40.3 1.8 fusion.34
  42.1 29.6 %all-gather.5.cloned.1.call-done = bf16[512,2048]{1,0:T(8,128)(2,1)} async-done(((bf16[512,512]{1,0:T(8,128)(2,1)}), bf16[512,2048]{1,0:T(8,128)(2,1)}) %all-gather.5.cloned.1.call-update) | async-done | bytes 2097168 | tf_op jit(solution)/shard_map/all_gather | solution.py:92
  71.7 2.1 fusion.6
  73.8 5.2 %fusion.49 = f32[512,1024]{1,0:T(8,128)S(1)} fusion(bf16[2048,1024]{1,0:T(8,128)(2,1)} %param.20, bf16[512,2048]{1,0:T(8,128)(2,1)} %all-gather.5.cloned.1.call-done, f32[2048]{0:T(1024)S(1)} %copy-done.12, f32[512]{0:T(512)S(1)} %add_rsqrt_fusion.2), kind=kOutput, calls=%fused_computation.93 | convolution fusion | flops 2151677952 | bytes 8398848 | tf_op jit(solution)/shard_map/dot_general | solution.py:32
  79.0 1.3 copy-done.2
  80.8 1.3 multiply_reduce_fusion
  82.1 1.0 copy.70
  83.2 2.7 multiply_reduce_fusion.2
  86.7 1.0 fusion.16
  88.4 2.2 fusion.2
  90.7 3.2 copy-done.1
  93.9 1.7 fusion.1
  95.6 8.8 %fusion.17 = bf16[128,8,512]{2,0,1:T(8,128)(2,1)} fusion(f32[8,512]{1,0:T(8,128)S(1)} %fusion.1, f32[8,512]{1,0:T(8,128)S(1)} %get-tuple-element.13, f32[512,512,8]{1,0,2:T(8,128)} %copy-done.1, pred[512,512]{0,1:T(8,128)(4,1)S(1)} %fusion.26, bf16[2048,128]{1,0:T(8,128)(2,1)} %param.22, bf16[512,2048]{1,0:T(8,128)(2,1)} %all-gather.5.cloned.1.call-done, ...), kind=kOutput, calls=%fused_computation.34 | convolution fusion | flops 820576256 | bytes 12363776 | tf_op jit(solution)/shard_map/kgst,tkd->skgd/dot_general | solution.py:61
  104.4 6.2 %convolution_convert_fusion.2 = bf16[512,2048]{1,0:T(8,128)(2,1)} fusion(bf16[512,1024]{0,1:T(8,128)(2,1)} %bitcast.94, bf16[1024,2048]{1,0:T(8,128)(2,1)} %param.23), kind=kOutput, calls=%fused_computation.26 | convolution fusion | flops 2148532224 | bytes 7340032 | tf_op jit(solution)/shard_map/dot_general | solution.py:96
  111.3 0.8 copy-done.4
  112.2 1.1 broadcast_add_fusion
  113.9 7.9 %fusion = pred[2048,128]{1,0:T(8,128)(4,1)S(1)} fusion(s32[128,8]{0,1:T(8,128)S(1)} %multiply_add_fusion), kind=kLoop, calls=%fused_computation.7 | loop fusion | flops 3932160 | bytes 266240 | tf_op jit(solution)/shard_map/reduce_or | solution.py:113
  121.8 47.9 %all-reduce.2.cloned.1.call-done = bf16[512,2048]{1,0:T(8,128)(2,1)} async-done(((bf16[512,2048]{1,0:T(8,128)(2,1)}), bf16[512,2048]{1,0:T(8,128)(2,1)}) %all-reduce.2.cloned.1.call-update) | async-done | bytes 2097168 | tf_op jit(solution)/shard_map/psum | solution.py:95
  169.7 1.5 multiply_reduce_fusion.1
  171.2 3.8 convolution_convert_fusion.1
  175.0 105.9 %all_to_all.10 = bf16[128,16,2048]{2,1,0:T(8,128)(2,1)S(1)} all-to-all(bf16[128,16,2048]{2,1,0:T(8,128)(2,1)S(1)} %bitcast.86), channel_id=1, replica_groups=mesh['exp'=32,'tp'=4] {'exp','tp'}, dimensions={0} | all-to-all | bytes 16777216 | tf_op jit(solution)/shard_map/all_to_all | solution.py:127
  280.9 16.0 %fusion.4 = f32[2048,1536]{1,0:T(8,128)} fusion(bf16[2048,2048]{1,0:T(8,128)(2,1)S(1)} %bitcast.88, bf16[1,2048,1536]{2,1,0:T(8,128)(2,1)S(1)} %bitcast.93), kind=kOutput, calls=%fused_computation.14 | convolution fusion | flops 12884901888 | bytes 27262976 | tf_op jit(solution)/shard_map/dot_general | solution.py:130
  296.9 13.9 %convolution_convert_fusion = bf16[2048,2048]{1,0:T(8,128)(2,1)} fusion(f32[2048,1536]{1,0:T(8,128)} %fusion.4, bf16[1,768,2048]{2,1,0:T(8,128)(2,1)S(1)} %copy-done), kind=kOutput, calls=%fused_computation.8 | convolution fusion | flops 6456082432 | bytes 24117248 | tf_op jit(solution)/shard_map/dot_general | solution.py:132
  310.8 5.9 %all-to-all-start.1 = ((bf16[128,16,2048]{2,1,0:T(8,128)(2,1)}), bf16[128,16,2048]{2,1,0:T(8,128)(2,1)}, u32[]{:S(2)}, u32[]{:S(2)}) async-start(bf16[128,16,2048]{2,1,0:T(8,128)(2,1)} %bitcast.87), calls=%async_computation.1 | async-start | bytes 16777216 | tf_op jit(solution)/shard_map/all_to_all | solution.py:133
  317.0 1.7 fusion.48
  318.8 6.8 %gather_fusion = f32[1024]{0:T(1024)S(1)} fusion(f32[128,128]{1,0:T(8,128)S(1)} %fusion.48, s32[1024]{0:T(1024)S(1)} %reshape.250), kind=kCustom, calls=%fused_computation | custom fusion | bytes 16384 | tf_op jit(solution)/shard_map/jit(take_along_axis)/gather | solution.py:102
  325.9 3.6 select_reduce_fusion
  329.5 95.3 %all-to-all-done.1 = bf16[128,16,2048]{2,1,0:T(8,128)(2,1)} async-done(((bf16[128,16,2048]{2,1,0:T(8,128)(2,1)}), bf16[128,16,2048]{2,1,0:T(8,128)(2,1)}, u32[]{:S(2)}, u32[]{:S(2)}) %all-to-all-start.1) | async-done | bytes 8388640 | tf_op jit(solution)/shard_map/all_to_all | solution.py:133
  424.8 5.8 %fusion.15 = bf16[128,2048]{1,0:T(8,128)(2,1)} fusion(bf16[2048,2048]{1,0:T(8,128)(2,1)} %bitcast.21, bf16[128,2048]{1,0:T(8,128)(2,1)} %select_reduce_fusion, bf16[512,2048]{1,0:T(8,128)(2,1)} %all-reduce.2.cloned.1.call-done, s32[]{:T(128)S(6)} %select_n.26, bf16[512,2048]{1,0:T(8,128)(2,1)} %all-gather.5.cloned.1.call-done), kind=kOutput, calls=%fused_computation.28 | convolution fusion | flops 1075052544 | bytes 10485764 | tf_op jit(solution)/shard_map/dot_general | solution.py:140
  (67 shorter events, 4.9 us)
Async XLA Ops:
  6.5 290.4 %copy-start = (bf16[1,768,2048]{2,1,0:T(8,128)(2,1)S(1)}, bf16[1,768,2048]{2,1,0:T(8,128)(2,1)}, u32[]{:S(2)}) copy-start(bf16[1,768,2048]{2,1,0:T(8,128)(2,1)} %param.31) | copy-start | bytes 9437188
  6.5 33.6 %copy-start.8 = (s32[1,512]{1,0:T(1,128)S(1)}, s32[1,512]{1,0:T(1,128)}, u32[]{:S(2)}) copy-start(s32[1,512]{1,0:T(1,128)} %param.19) | copy-start | bytes 6148
  6.5 30.1 %all-gather.3.cloned.1.call-start = ((), (), s32[]{:S(2)}) async-start(), calls=%async_computation.2 | async-start | bytes 1638400 | tf_op jit(solution)/shard_map/all_gather | solution.py:86
  7.3 64.4 %all-gather.5.cloned.1.call-start = ((), (), s32[]{:S(2)}) async-start(), calls=%async_computation.3 | async-start | bytes 2621440 | tf_op jit(solution)/shard_map/all_gather | solution.py:92
  8.2 65.5 %copy-start.12 = (f32[2048]{0:T(1024)S(1)}, f32[2048]{0:T(1024)}, u32[]{:S(2)}) copy-start(f32[2048]{0:T(1024)} %param.24) | copy-start | bytes 24580
  40.0 129.7 %all-reduce.2.cloned.1.call-start = ((), (), s32[]{:S(2)}) async-start(), calls=%async_computation.4 | async-start | bytes 4194304 | tf_op jit(solution)/shard_map/psum | solution.py:95
  79.0 1.4 copy-start.2
  80.8 5.2 %copy-start.10 = (f32[128]{0:T(128)S(1)}, f32[128]{0:T(128)}, u32[]{:S(2)}) copy-start(f32[128]{0:T(128)} %param.26) | copy-start | bytes 1540
  80.8 5.9 %copy-start.11 = (f32[128]{0:T(128)S(1)}, f32[128]{0:T(128)}, u32[]{:S(2)}) copy-start(f32[128]{0:T(128)} %param.25) | copy-start | bytes 1540
  83.2 3.5 copy-start.3
  83.2 4.4 %copy-start.5 = (f32[512,64]{1,0:T(8,128)S(1)}, f32[512,64]{1,0:T(8,128)}, u32[]{:S(2)}) copy-start(f32[512,64]{1,0:T(8,128)} %get-tuple-element.9) | copy-start | bytes 393220
  83.2 4.4 %copy-start.6 = (f32[512,64]{1,0:T(8,128)S(1)}, f32[512,64]{1,0:T(8,128)}, u32[]{:S(2)}) copy-start(f32[512,64]{1,0:T(8,128)} %get-tuple-element.10) | copy-start | bytes 393220
  90.7 3.2 copy-start.1
  104.4 6.3 %copy-start.7 = (s32[128,8]{0,1:T(8,128)S(1)}, s32[128,8]{0,1:T(8,128)}, u32[]{:S(2)}) copy-start(s32[128,8]{0,1:T(8,128)} %param.29) | copy-start | bytes 12292
  110.7 60.5 %copy-start.9 = (f32[2048]{0:T(1024)S(1)}, f32[2048]{0:T(1024)}, u32[]{:S(2)}) copy-start(f32[2048]{0:T(1024)} %param.27) | copy-start | bytes 24580
  111.3 0.8 copy-start.4
  171.2 109.7 %slice-start = ((s8[6291456]{0:T(1024)(128)(4,1)}), s8[4194304]{0:T(1024)(128)(4,1)S(1)}, s32[]{:S(2)}) async-start(s8[6291456]{0:T(1024)(128)(4,1)} %bitcast.92), calls=%async_computation.5 | async-start | bytes 8388608
  175.0 105.9 %slice-start.1 = ((s8[6291456]{0:T(1024)(128)(4,1)}), s8[2097152]{0:T(1024)(128)(4,1)S(1)}, s32[]{:S(2)}) async-start(s8[6291456]{0:T(1024)(128)(4,1)} %bitcast.92), calls=%async_computation.6 | async-start | bytes 4194304
  310.8 114.0 %all-to-all-start.1 = ((bf16[128,16,2048]{2,1,0:T(8,128)(2,1)}), bf16[128,16,2048]{2,1,0:T(8,128)(2,1)}, u32[]{:S(2)}, u32[]{:S(2)}) async-start(bf16[128,16,2048]{2,1,0:T(8,128)(2,1)} %bitcast.87), calls=%async_computation.1 | async-start | bytes 16777216 | tf_op jit(solution)/shard_map/all_to_all | solution.py:133
Sparse Core Ops, SparseCore 0:
  9.0 27.5 all-gather.2
  40.1 31.4 all-gather.4
  110.8 58.8 all-reduce.1
where the time goes:
time: 443 us; the launch traced here: 437 us
  waiting for transfers between devices  202 us (46%)
  blocking collectives  106 us (24%)
  matrix products  69.8 us (16%)
  other arithmetic  24.3 us (5%)
  local copies, waits for them, and re-layouts  15.8 us (4%)
  between operations  13.6 us (3%)
  starting transfers between devices  6.01 us (1%)
    all_to_all x1, blocking collectives, on_device(): lax.all_to_all(outgoing, ('exp', 'tp'), split_axis=0, concat_axis=0, tile...  106 us
    all_to_all x1, waiting for transfers between devices, on_device(): lax.all_to_all(expert_out.reshape(source, slot_count, width_in), ('exp',...  95.3 us
    psum x1, waiting for transfers between devices, on_device(): lax.psum(jnp.dot(context, w_o, preferred_element_type=jnp.float32).astype...  47.9 us
    all_gather x1, waiting for transfers between devices, on_device(): x_seq = lax.all_gather(columns, 'tp', axis=1, tiled=True)  29.6 us
    all_gather x1, waiting for transfers between devices, on_device(): seq_audio = lax.all_gather(audio_feats, 'tp', axis=0, tiled=True)  28.4 us
    dot_general x1, matrix products, on_device(): jnp.dot(flat_rows, w_gate_up[0], preferred_element_type=jnp.float32)  16 us
    dot_general x1, matrix products, on_device(): jnp.dot(hidden, w_down[0], preferred_element_type=jnp.float32)  13.9 us
  transfers between devices with their start and end apart: 4, of which 4 were waited for; matrix products, arithmetic and copies ran while one was open for 6% of the time, Pallas kernels for 0%

commit v1 on v0

v1 whole, which is shorter than its diff:
```python
import jax
import jax.numpy as jnp
from jax import lax
from jax.experimental import pallas as pl
from jax.experimental.pallas import tpu as pltpu
from jax.sharding import PartitionSpec as P

EPSILON = 1e-06
ROPE_BASE = 1000000.0
F32 = jnp.float32
BF16 = jnp.bfloat16
VMEM_BYTES = 48 * 1024 * 1024


def whole(count):
    return [pl.BlockSpec(memory_space=pltpu.VMEM)] * count


def shift(value, by):
    size = lax.axis_size("tp")
    return lax.ppermute(value, "tp", [(i, (i + by) % size) for i in range(size)])


def rope_tables(seq_len, head_dim):
    half_dim = head_dim // 2
    inv_freq = ROPE_BASE ** (-(jnp.arange(half_dim, dtype=F32) * 2.0) / head_dim)
    angles = jnp.arange(seq_len, dtype=F32)[:, None] * inv_freq[None, :]
    cos, sin = jnp.cos(angles), jnp.sin(angles)
    return jnp.concatenate([cos, cos], axis=1), jnp.concatenate([-sin, sin], axis=1)


def layer_kernel(*refs, first):
    order, own, left, right, opposite = refs[:5]
    refs = refs[5:]
    if first:
        past_keys, past_values = refs[:2]
        refs = refs[2:]
    (gain, w_q, w_k, w_v, w_o, q_gain, k_gain, cos, sin, seg_col, seg_row,
     to_right, to_left, to_opposite, to_own, keys_out, values_out,
     normed, queries, keys, values, context) = refs
    count, width = own.shape
    feat_dim = w_q.shape[0]
    head_dim = w_k.shape[1]
    heads = queries.shape[0]
    block = 128

    pieces = [piece[...].astype(F32) for piece in (own, left, right, opposite)]
    squares = sum(jnp.sum(piece * piece, axis=1, keepdims=True) for piece in pieces)
    scale = lax.rsqrt(squares / feat_dim + EPSILON)
    for place, piece in enumerate(pieces):
        at = order[place]
        columns = pl.ds(pl.multiple_of(at * width, width), width)
        normed[:, columns] = (piece * scale * gain[pl.ds(at, 1), :]).astype(BF16)

    here = pl.ds(first, count)
    turn_cos, turn_sin = cos[here, :], sin[here, :]

    def head_of(raw, head_gain):
        squares = jnp.mean(raw * raw, axis=1, keepdims=True)
        raw = raw * lax.rsqrt(squares + EPSILON) * head_gain[...]
        return (raw * turn_cos + pltpu.roll(raw, head_dim // 2, 1) * turn_sin).astype(BF16)

    if first:
        keys[:first, :] = past_keys[...]
        values[:first, :] = past_values[...]
    new_keys = head_of(jnp.dot(normed[...], w_k[...], preferred_element_type=F32), k_gain)
    new_values = jnp.dot(normed[...], w_v[...], preferred_element_type=F32).astype(BF16)
    keys[here, :] = new_keys
    values[here, :] = new_values
    keys_out[...] = new_keys
    values_out[...] = new_values
    for pair in range(heads // 2):
        raw = jnp.dot(
            normed[...], w_q[:, pl.ds(pair * 2 * head_dim, 2 * head_dim)],
            preferred_element_type=F32,
        )
        for one in range(2):
            queries[2 * pair + one] = head_of(raw[:, one * head_dim : (one + 1) * head_dim], q_gain)

    for start in range(0, count, block):
        span = first + start + block
        row_at = first + start + lax.broadcasted_iota(jnp.int32, (block, span), 0)
        col_at = lax.broadcasted_iota(jnp.int32, (block, span), 1)
        same = seg_col[pl.ds(first + start, block), :] == seg_row[:, :span]
        allowed = same & (col_at <= row_at)
        for head in range(heads):
            scores = lax.dot_general(
                queries[head, pl.ds(start, block), :], keys[:span, :], (((1,), (1,)), ((), ())),
                preferred_element_type=F32,
            ) * (float(head_dim) ** -0.5)
            scores = jnp.where(allowed, scores, -1e30)
            expo = jnp.exp(scores - jnp.max(scores, axis=1, keepdims=True))
            total = jnp.sum(expo, axis=1, keepdims=True)
            mixed = jnp.dot(expo.astype(BF16), values[:span, :], preferred_element_type=F32)
            context[pl.ds(start, block), pl.ds(head * head_dim, head_dim)] = (
                mixed / total
            ).astype(BF16)

    for place, out in ((2, to_right), (1, to_left), (3, to_opposite), (0, to_own)):
        columns = pl.ds(pl.multiple_of(order[place] * width, width), width)
        out[...] = jnp.dot(context[...], w_o[:, columns], preferred_element_type=F32).astype(BF16)


def run_layer(order, parts, past, first, gain, w_q, w_k, w_v, w_o, q_gain, k_gain, cos, sin, seg):
    count, width = parts[0].shape
    feat_dim = w_q.shape[0]
    head_dim = w_k.shape[1]
    heads = w_q.shape[1] // head_dim
    span = first + count
    piece = jax.ShapeDtypeStruct((count, width), BF16)
    kv = jax.ShapeDtypeStruct((count, head_dim), BF16)
    operands = [*parts, *past, gain, w_q, w_k, w_v, w_o, q_gain, k_gain, cos, sin, *seg]

    def kernel(*refs):
        layer_kernel(*refs, first=first)

    return pl.pallas_call(
        kernel,
        in_specs=[pl.BlockSpec(memory_space=pltpu.SMEM)] + whole(len(operands)),
        out_specs=whole(6),
        out_shape=(piece,) * 4 + (kv,) * 2,
        scratch_shapes=[
            pltpu.VMEM((count, feat_dim), BF16),
            pltpu.VMEM((heads, count, head_dim), BF16),
            pltpu.VMEM((span, head_dim), BF16),
            pltpu.VMEM((span, head_dim), BF16),
            pltpu.VMEM((count, heads * head_dim), BF16),
        ],
        compiler_params=pltpu.CompilerParams(vmem_limit_bytes=VMEM_BYTES),
        cost_estimate=pl.CostEstimate(
            flops=4 * count * feat_dim * (heads + 1) * head_dim
            + 4 * count * span * heads * head_dim,
            transcendentals=count * span * heads,
            bytes_accessed=4 * feat_dim * (heads + 1) * head_dim + 16 * count * width,
        ),
        name="layer",
    )(order, *operands)


def one_hot(places, cap):
    rows, tokens = places.shape
    slot = lax.broadcasted_iota(jnp.int32, (rows, cap, tokens), 1).astype(F32)
    return jnp.broadcast_to(places[:, None, :], slot.shape) == slot


def dispatch_kernel(columns, from_left, from_right, from_opposite, own, places, out, hidden, rounded):
    @pl.when(pl.program_id(0) == 0)
    def _():
        total = columns[...].astype(F32)
        for piece in (own, from_left, from_right, from_opposite):
            total = total + piece[...].astype(F32)
        hidden[...] = total
        rounded[...] = total.astype(BF16)

    blocks, group, tokens = places.shape
    cap = out.shape[1] // blocks
    for block in range(blocks):
        chosen = one_hot(places[block], cap).astype(F32).reshape(group * cap, tokens).astype(BF16)
        rows = jnp.dot(
            chosen, rounded[pl.ds(block * tokens, tokens), :], preferred_element_type=F32
        ).astype(BF16)
        out[:, pl.ds(block * cap, cap), :] = rows.reshape(group, cap, rows.shape[1])


def run_dispatch(columns, pieces, places, cap):
    count, width = columns.shape
    blocks, experts, tokens = places.shape
    group = 16
    fixed = pl.BlockSpec((count, width), lambda i: (0, 0))
    return pl.pallas_call(
        dispatch_kernel,
        grid=(experts // group,),
        in_specs=[fixed] * 5 + [pl.BlockSpec((blocks, group, tokens), lambda i: (0, i, 0))],
        out_specs=[pl.BlockSpec((group, blocks * cap, width), lambda i: (i, 0, 0)), fixed],
        out_shape=(
            jax.ShapeDtypeStruct((experts, blocks * cap, width), BF16),
            jax.ShapeDtypeStruct((count, width), F32),
        ),
        scratch_shapes=[pltpu.VMEM((count, width), BF16)],
        compiler_params=pltpu.CompilerParams(vmem_limit_bytes=VMEM_BYTES),
        cost_estimate=pl.CostEstimate(
            flops=2 * experts * cap * count * width, transcendentals=0,
            bytes_accessed=2 * experts * blocks * cap * width,
        ),
        name="dispatch",
    )(columns, *pieces, places)


def expert_kernel(rows, gain, w_gate_up, w_down, out, normed):
    groups, parts, slots, width = rows.shape
    count = groups * slots
    feat_dim = parts * width
    inner = w_down.shape[0]
    pieces = [rows[:, part].reshape(count, width).astype(F32) for part in range(parts)]
    squares = sum(jnp.sum(piece * piece, axis=1, keepdims=True) for piece in pieces)
    scale = lax.rsqrt(squares / feat_dim + EPSILON)
    for part, piece in enumerate(pieces):
        normed[:, pl.ds(part * width, width)] = (
            piece * scale * gain[pl.ds(part, 1), :]
        ).astype(BF16)
    both = jnp.dot(normed[...], w_gate_up[...], preferred_element_type=F32)
    gate, up = both[:, :inner], both[:, inner:]
    hidden = (gate * jax.nn.sigmoid(gate) * up).astype(BF16)
    for part in range(parts):
        result = jnp.dot(
            hidden, w_down[:, pl.ds(part * width, width)], preferred_element_type=F32
        )
        out[:, part] = result.astype(BF16).reshape(groups, slots, width)


def run_experts(arrived, gain, w_gate_up, w_down):
    sources, parts, slots, width = arrived.shape
    feat_dim, double = w_gate_up.shape
    groups = 8
    moving = pl.BlockSpec((groups, parts, slots, width), lambda i: (i, 0, 0, 0))

    def fixed(shape):
        return pl.BlockSpec(shape, lambda i: (0, 0), pipeline_mode=pl.Buffered(1))

    return pl.pallas_call(
        expert_kernel,
        grid=(sources // groups,),
        in_specs=[moving, fixed(gain.shape), fixed(w_gate_up.shape), fixed(w_down.shape)],
        out_specs=moving,
        out_shape=jax.ShapeDtypeStruct(arrived.shape, BF16),
        scratch_shapes=[pltpu.VMEM((groups * slots, feat_dim), BF16)],
        compiler_params=pltpu.CompilerParams(vmem_limit_bytes=VMEM_BYTES),
        cost_estimate=pl.CostEstimate(
            flops=3 * sources * slots * feat_dim * double,
            transcendentals=sources * slots * double // 2,
            bytes_accessed=4 * sources * slots * feat_dim + 3 * feat_dim * double,
        ),
        name="experts",
    )(arrived, gain, w_gate_up, w_down)


def combine_kernel(returned, gates, places, hidden, out, total):
    step = pl.program_id(0)

    @pl.when(step == 0)
    def _():
        total[...] = hidden[...]

    blocks, group, tokens = places.shape
    cap = returned.shape[1] // blocks
    for block in range(blocks):
        weights = jnp.where(
            one_hot(places[block], cap),
            jnp.broadcast_to(gates[block][:, None, :], (group, cap, tokens)),
            0.0,
        ).reshape(group * cap, tokens).astype(BF16)
        rows = returned[:, pl.ds(block * cap, cap), :].reshape(group * cap, -1)
        total[pl.ds(block * tokens, tokens), :] += lax.dot_general(
            weights, rows, (((0,), (0,)), ((), ())), preferred_element_type=F32
        )

    @pl.when(step == pl.num_programs(0) - 1)
    def _():
        out[...] = total[...].astype(BF16)


def run_combine(returned, gates, places, hidden):
    count, width = hidden.shape
    blocks, experts, tokens = places.shape
    group = 16
    table = pl.BlockSpec((blocks, group, tokens), lambda i: (0, i, 0))
    fixed = pl.BlockSpec((count, width), lambda i: (0, 0))
    return pl.pallas_call(
        combine_kernel,
        grid=(experts // group,),
        in_specs=[
            pl.BlockSpec((group, returned.shape[1], width), lambda i: (i, 0, 0)), table, table, fixed
        ],
        out_specs=fixed,
        out_shape=jax.ShapeDtypeStruct((count, width), BF16),
        scratch_shapes=[pltpu.VMEM((count, width), F32)],
        compiler_params=pltpu.CompilerParams(vmem_limit_bytes=VMEM_BYTES),
        cost_estimate=pl.CostEstimate(
            flops=2 * returned.size * tokens, transcendentals=0, bytes_accessed=2 * returned.size
        ),
        name="combine",
    )(returned, gates, places, hidden)


def join_kernel(order, own, left, right, opposite, out):
    width = own.shape[1]
    for place, piece in enumerate((own, left, right, opposite)):
        out[:, pl.ds(pl.multiple_of(order[place] * width, width), width)] = piece[...]


def run_join(order, pieces):
    count, width = pieces[0].shape
    return pl.pallas_call(
        join_kernel,
        in_specs=[pl.BlockSpec(memory_space=pltpu.SMEM)] + whole(4),
        out_specs=whole(1)[0],
        out_shape=jax.ShapeDtypeStruct((count, 4 * width), BF16),
        name="join",
    )(order, *pieces)


def on_device(
    audio_feats, w_audio, b_audio, segments, w_q, w_k, w_v, w_o, attn_gain, q_gain, k_gain,
    moe_gain, w_router, routes, w_gate_up, w_down,
):
    me = lax.axis_index("tp")
    tp_size = lax.axis_size("tp")
    tok_rows = audio_feats.shape[0]
    feat_dim = b_audio.shape[0]
    seq_len = segments.shape[1]
    head_dim = q_gain.shape[0]
    experts = w_router.shape[1]
    top_count = routes.shape[1]
    width = w_audio.shape[1]
    slot_cap = max(4, 2 * tok_rows * top_count // experts)
    order = lax.rem(me + jnp.array([0, 3, 1, 2], jnp.int32), tp_size)

    def exchange(value):
        return [value, shift(value, 1), shift(value, -1), shift(value, 2)]

    def in_order(value):
        stack = jnp.zeros((tp_size,) + value.shape, value.dtype)
        for place, piece in enumerate(exchange(value)):
            stack = lax.dynamic_update_slice_in_dim(stack, piece[None], order[place], 0)
        return stack

    seq_audio = in_order(audio_feats).reshape(seq_len, -1)

    expert_ids = jnp.arange(experts, dtype=jnp.int32)
    named = jnp.any(routes.T[:, None, :] == expert_ids[None, :, None], axis=0)
    token_ids = jnp.arange(tok_rows, dtype=jnp.int32)
    earlier = (token_ids[:, None] < token_ids[None, :]).astype(BF16)
    places = jnp.dot(named.astype(BF16), earlier, preferred_element_type=F32)
    places = in_order(jnp.where(named, places, -1.0).astype(BF16)).astype(F32)

    bias_part = lax.dynamic_slice_in_dim(b_audio, me * width, width, 0)
    columns = (jnp.dot(seq_audio, w_audio, preferred_element_type=F32) + bias_part).astype(BF16)

    cos, sin = rope_tables(seq_len, head_dim)
    seg = (segments.reshape(seq_len, 1), segments)
    router_part = lax.dynamic_slice_in_dim(w_router, me * width, width, 0)
    gain_part = lax.dynamic_slice_in_dim(moe_gain, me * width, width, 0)
    by_device = (tp_size, width)

    def gates_of(hidden, chunk_places):
        count = hidden.shape[0]
        blocks = chunk_places.shape[0]
        scaled = (hidden * gain_part).astype(BF16)
        partial = jnp.dot(scaled, router_part, preferred_element_type=F32)
        squares = jnp.sum(hidden * hidden, axis=1).reshape(blocks, tok_rows)
        squares = jnp.pad(squares, ((0, 8 - blocks), (0, 0)))
        packed = sum(exchange(jnp.concatenate([partial, squares], axis=0)))
        scale = lax.rsqrt(packed[count : count + blocks] / feat_dim + EPSILON)
        logits = packed[:count].reshape(blocks, tok_rows, experts).transpose(0, 2, 1)
        logits = logits * scale[:, None, :]
        here = chunk_places >= 0
        peak = jnp.max(jnp.where(here, logits, -jnp.inf), axis=1, keepdims=True)
        expo = jnp.where(here, jnp.exp(jnp.minimum(logits - peak, 0.0)), 0.0)
        gates = expo / jnp.sum(expo, axis=1, keepdims=True)
        return gates.astype(BF16).astype(F32)

    starts = (0, tok_rows, seq_len)
    past, pending = (), []
    for first, end in zip(starts[:-1], starts[1:]):
        chunk = columns[first:end]
        parts = exchange(chunk)
        *pieces, keys, values = run_layer(
            order, parts, past, first, attn_gain.reshape(by_device), w_q, w_k, w_v, w_o,
            q_gain[None], k_gain[None], cos, sin, seg,
        )
        past = (keys, values)
        to_right, to_left, to_opposite, mine = pieces
        summed = [shift(to_right, 1), shift(to_left, -1), shift(to_opposite, 2), mine]
        chunk_places = places[first // tok_rows : end // tok_rows]
        outgoing, hidden = run_dispatch(chunk, summed, chunk_places, slot_cap)
        arrived = lax.all_to_all(outgoing, ("exp", "tp"), 0, 0, tiled=True)
        pending.append((arrived, hidden, chunk_places))

    finished = []
    for arrived, hidden, chunk_places in pending:
        _, slots, _ = arrived.shape
        results = run_experts(
            arrived.reshape(-1, tp_size, slots, width), moe_gain.reshape(by_device),
            w_gate_up[0], w_down[0],
        )
        returned = lax.all_to_all(
            results.reshape(arrived.shape), ("exp", "tp"), 0, 0, tiled=True
        )
        gates = gates_of(hidden, chunk_places)
        finished.append(run_combine(returned, gates, chunk_places, hidden))

    blocks = jnp.concatenate(finished, axis=0).reshape(tp_size, tok_rows, width)

    def block_of(place):
        return lax.dynamic_index_in_dim(blocks, order[place], 0, keepdims=False)

    gathered = [
        block_of(0), shift(block_of(2), 1), shift(block_of(1), -1), shift(block_of(3), 2)
    ]
    return run_join(order, gathered)


def solution(mesh):
    in_specs = (
        P(("exp", "tp"), None),
        P(None, "tp"),
        P(),
        P("exp", None),
        P(None, "tp"),
        P(None, "tp"),
        P(None, "tp"),
        P("tp", None),
        P(),
        P(),
        P(),
        P(),
        P(),
        P(("exp", "tp"), None),
        P(("exp", "tp"), None, None),
        P(("exp", "tp"), None, None),
    )
    out_specs = P(("exp", "tp"), None)
    return jax.shard_map(
        on_device, mesh=mesh, in_specs=in_specs, out_specs=out_specs, check_vma=False
    )
```

time: 443 us -> 412 us (0.930)
  blocking collectives: 106 us -> 0 us
  Pallas kernels: 0 us -> 70.2 us
  starting transfers between devices: 6.01 us -> 71.3 us
  matrix products: 69.8 us -> 5.32 us
  waiting for transfers between devices: 202 us -> 225 us
  other arithmetic: 24.3 us -> 5.99 us
  local copies, waits for them, and re-layouts: 15.8 us -> 21.8 us
  between operations: 13.6 us -> 7.98 us
    ppermute x0 -> x27, waiting for transfers between devices: none -> 150 us  [shift(): lax.ppermute(value, 'tp', [(i, (i + by) % size) for i in range(size)])]
    all_to_all x1 -> x0, blocking collectives: 106 us -> none  [on_device(): lax.all_to_all(outgoing, ('exp', 'tp'), split_axis=0, concat_axis=0, tile...]
    pallas_call x0 -> x9, Pallas kernels: none -> 70.2 us  [the longest x2 31.3 us: run_experts(): pl.pallas_call(expert_kernel, grid=(sources // groups,), in_specs=[moving...]
    dot_general x11 -> x4, matrix products: 69.8 us -> 5.32 us  [the longest x2 2.31 us: gates_of(): partial = jnp.dot(scaled, router_part, preferred_element_type=F32)]
    all_gather x2 -> x0, waiting for transfers between devices: 58 us -> none  [the longest x1 29.6 us: on_device(): x_seq = lax.all_gather(columns, 'tp', axis=1, tiled=True)]
    psum x1 -> x0, waiting for transfers between devices: 47.9 us -> none  [on_device(): lax.psum(jnp.dot(context, w_o, preferred_element_type=jnp.float32).astype...]
    ppermute x0 -> x27, starting transfers between devices: none -> 39.6 us  [shift(): lax.ppermute(value, 'tp', [(i, (i + by) % size) for i in range(size)])]
    all_to_all x1 -> x4, starting transfers between devices: 5.93 us -> 31.7 us  [the longest x2 17.7 us: on_device(): arrived = lax.all_to_all(outgoing, ('exp', 'tp'), 0, 0, tiled=True)]
  transfers between devices with their start and end apart: 4 -> 31, of which waited for: 4 -> 14; matrix products, arithmetic and copies ran while one was open for 6% -> 5% of each run, Pallas kernels for 0% -> 15%
where the time goes in v1:
time: 412 us; the launch traced here: 408 us
  waiting for transfers between devices  225 us (55%)
  starting transfers between devices  71.3 us (17%)
  Pallas kernels  70.2 us (17%)
  local copies, waits for them, and re-layouts  21.8 us (5%)
  between operations  7.98 us (2%)
  other arithmetic  5.99 us (1%)
  matrix products  5.32 us (1%)
    ppermute x27, waiting for transfers between devices, shift(): lax.ppermute(value, 'tp', [(i, (i + by) % size) for i in range(size)])  150 us
    all_to_all x2, waiting for transfers between devices, on_device(): arrived = lax.all_to_all(outgoing, ('exp', 'tp'), 0, 0, tiled=True)  68.2 us
    ppermute x27, starting transfers between devices, shift(): lax.ppermute(value, 'tp', [(i, (i + by) % size) for i in range(size)])  39.6 us
    pallas_call x2, Pallas kernels, run_experts(): pl.pallas_call(expert_kernel, grid=(sources // groups,), in_specs=[moving...  31.3 us
    pallas_call x2, Pallas kernels, run_layer(): pl.pallas_call(kernel, in_specs=[pl.BlockSpec(memory_space=pltpu.SMEM)] +...  21.1 us
    all_to_all x2, starting transfers between devices, on_device(): arrived = lax.all_to_all(outgoing, ('exp', 'tp'), 0, 0, tiled=True)  17.7 us
    all_to_all x2, starting transfers between devices, on_device(): lax.all_to_all(results.reshape(arrived.shape), ('exp', 'tp'), 0, 0, tiled...  14 us
    unnamed x74, local copies, waits for them, and re-layouts  11.5 us
  transfers between devices with their start and end apart: 31, of which 14 were waited for; matrix products, arithmetic and copies ran while one was open for 5% of the time, Pallas kernels for 15%

profile of v1, /device:TPU:0, one launch (start us, length us, event | category | flops | bytes accessed | tf_op | source)
XLA Modules:
  0.0 407.8 jit_solution(9099776368759956109)
XLA Ops:
  2.0 2.2 collective-permute-start.1
  11.7 2.2 collective-permute-start.10
  26.7 2.2 fusion.2
  30.1 2.9 collective-permute-start.4
  36.9 2.5 collective-permute-done.5.refs_4_
  39.5 7.2 %layer.2 = (bf16[128,512]{1,0:T(8,128)(2,1)S(1)}, bf16[128,512]{1,0:T(8,128)(2,1)S(1)}, bf16[128,512]{1,0:T(8,128)(2,1)S(1)}, bf16[128,512]{1,0:T(8,128)(2,1)S(1...) custom-call(s32[4]{0:T(128)S(1)} %compare_select_fusion.refs_0_.order, ...), custom_call_target="tpu_custom_call" | custom-call | flops 1275068416 | bytes 10485760 | tf_op jit(solution)/shard_map/layer/pallas_call | solution.py:117
  46.8 3.2 collective-permute-start.7
  50.7 3.6 collective-permute-done.6.from_left
  54.3 2.2 collective-permute-done.8.from_opposite
  59.7 8.1 %all-to-all-start = ((bf16[128,16,512]{2,1,0:T(8,128)(2,1)}), bf16[128,16,512]{2,1,0:T(8,128)(2,1)S(1)}, u32[]{:S(2)}, u32[]{:S(2)}) async-start(bf16[128,16,512]{2,1,0:T(8,128)(2,1)} %copy-done.2), calls=%async_computation | async-start | bytes 4194304 | tf_op jit(solution)/shard_map/all_to_all | solution.py:376
  73.8 28.3 %collective-permute-done.15.refs_2_ = bf16[384,512]{1,0:T(8,128)(2,1)S(1)} collective-permute-done((bf16[384,512]{1,0:T(8,128)(2,1)S(1)}, bf16[384,512]{1,0:T(8,128)(2,1)S(1)}, u32[]{:S(2)}, u32[]{:S(2)}) %collective-permute-start.15) | collective-permute-done | bytes 393248 | tf_op jit(solution)/shard_map/ppermute | solution.py:21
  102.1 8.7 %collective-permute-done.17.refs_4_ = bf16[384,512]{1,0:T(8,128)(2,1)S(1)} collective-permute-done((bf16[384,512]{1,0:T(8,128)(2,1)S(1)}, bf16[384,512]{1,0:T(8,128)(2,1)S(1)}, u32[]{:S(2)}, u32[]{:S(2)}) %collective-permute-start.17) | collective-permute-done | bytes 393248 | tf_op jit(solution)/shard_map/ppermute | solution.py:21
  113.7 13.9 %layer.3 = (bf16[384,512]{1,0:T(8,128)(2,1)S(1)}, bf16[384,512]{1,0:T(8,128)(2,1)S(1)}, bf16[384,512]{1,0:T(8,128)(2,1)S(1)}, bf16[384,512]{1,0:T(8,128)(2,1)S(1...) custom-call(s32[4]{0:T(128)S(1)} %compare_select_fusion.refs_0_.order, ...), custom_call_target="tpu_custom_call" | custom-call | flops 4429185024 | bytes 12582912 | tf_op jit(solution)/shard_map/layer/pallas_call | solution.py:117
  128.6 2.4 collective-permute-start.19
  131.0 17.4 %collective-permute-done.18.from_left = bf16[384,512]{1,0:T(8,128)(2,1)S(1)} collective-permute-done((bf16[384,512]{1,0:T(8,128)(2,1)S(1)}, bf16[384,512]{1,0:T(8,128)(2,1)S(1)}, u32[]{:S(2)}, u32[]{:S(2)}) %collective-permute-start.18) | collective-permute-done | bytes 393248 | tf_op jit(solution)/shard_map/ppermute | solution.py:21
  148.4 5.8 %dispatch.3 = (bf16[128,48,512]{2,1,0:T(8,128)(2,1)}, f32[384,512]{1,0:T(8,128)S(1)}) custom-call(bf16[384,512]{1,0:T(8,128)(2,1)S(1)} %slice.60.refs_1_.columns, bf16[384,512]{1,0:T(8,128)(2,1)S(1)} %collective-permute-done.18.from_left, bf16[384,512]{1,0:T(8,128)(2,1)S(1)} %collective-permute-done.19.from_right, ...), custom_call_target="tpu_custom_call" | custom-call | flops 805306368 | bytes 6291456 | tf_op jit(solution)/shard_map/dispatch/pallas_call | solution.py:170
  154.2 9.6 %all-to-all-start.2 = ((bf16[128,48,512]{2,1,0:T(8,128)(2,1)}), bf16[128,48,512]{2,1,0:T(8,128)(2,1)}, u32[]{:S(2)}, u32[]{:S(2)}) async-start(bf16[128,48,512]{2,1,0:T(8,128)(2,1)} %get-tuple-element.31), calls=%async_computation.2 | async-start | bytes 12582912 | tf_op jit(solution)/shard_map/all_to_all | solution.py:376
  163.9 10.2 %experts.2 = bf16[32,4,16,512]{3,2,1,0:T(8,128)(2,1)S(1)} custom-call(bf16[32,4,16,512]{3,2,1,0:T(8,128)(2,1)S(1)} %bitcast.78, f32[4,512]{1,0:T(4,128)S(1)} %reshape.71.gain, bf16[2048,1536]{1,0:T(8,128)(2,1)} %bitcast.95, bf16[768,2048]{1,0:T(8,128)(2,1)} %bitcast.85), custom_call_target="tpu_custom_call" | custom-call | flops 4831838208 | bytes 13631488 | tf_op jit(solution)/shard_map/experts/pallas_call | solution.py:220
  175.4 68.2 %all-to-all-done.2 = bf16[128,48,512]{2,1,0:T(8,128)(2,1)} async-done(((bf16[128,48,512]{2,1,0:T(8,128)(2,1)}), bf16[128,48,512]{2,1,0:T(8,128)(2,1)}, u32[]{:S(2)}, u32[]{:S(2)}) %all-to-all-start.2) | async-done | bytes 6291488 | tf_op jit(solution)/shard_map/all_to_all | solution.py:376
  243.6 8.0 %all-to-all-start.1 = ((bf16[128,16,512]{2,1,0:T(8,128)(2,1)}), bf16[128,16,512]{2,1,0:T(8,128)(2,1)S(1)}, u32[]{:S(2)}, u32[]{:S(2)}) async-start(bf16[128,16,512]{2,1,0:T(8,128)(2,1)} %bitcast.79), calls=%async_computation.1 | async-start | bytes 4194304 | tf_op jit(solution)/shard_map/all_to_all | solution.py:386
  253.5 21.1 %experts.3 = bf16[32,4,48,512]{3,2,1,0:T(8,128)(2,1)} custom-call(bf16[32,4,48,512]{3,2,1,0:T(8,128)(2,1)} %bitcast.24.rows, f32[4,512]{1,0:T(4,128)S(1)} %reshape.71.gain, bf16[2048,1536]{1,0:T(8,128)(2,1)} %bitcast.96, bf16[768,2048]{1,0:T(8,128)(2,1)S(1)} %bitcast.86), custom_call_target="tpu_custom_call" | custom-call | flops 14495514624 | bytes 22020096 | tf_op jit(solution)/shard_map/experts/pallas_call | solution.py:220
  274.5 7.2 %all-to-all-done.1.returned = bf16[128,16,512]{2,1,0:T(8,128)(2,1)S(1)} async-done(((bf16[128,16,512]{2,1,0:T(8,128)(2,1)}), bf16[128,16,512]{2,1,0:T(8,128)(2,1)S(1)}, u32[]{:S(2)}, u32[]{:S(2)}) %all-to-all-start.1) | async-done | bytes 2097184 | tf_op jit(solution)/shard_map/all_to_all | solution.py:386
  281.8 6.0 %all-to-all-start.3 = ((bf16[128,48,512]{2,1,0:T(8,128)(2,1)}), bf16[128,48,512]{2,1,0:T(8,128)(2,1)}, u32[]{:S(2)}, u32[]{:S(2)}) async-start(bf16[128,48,512]{2,1,0:T(8,128)(2,1)} %bitcast.87), calls=%async_computation.3 | async-start | bytes 12582912 | tf_op jit(solution)/shard_map/all_to_all | solution.py:386
  290.3 2.2 collective-permute-start.13
  294.1 64.2 %collective-permute-done.12 = f32[136,128]{0,1:T(8,128)S(1)} collective-permute-done((f32[136,128]{0,1:T(8,128)S(1)}, f32[136,128]{0,1:T(8,128)S(1)}, u32[]{:S(2)}, u32[]{:S(2)}) %collective-permute-start.12) | collective-permute-done | bytes 69664 | tf_op jit(solution)/shard_map/ppermute | solution.py:21
  358.3 6.7 %collective-permute-done.14 = f32[136,128]{0,1:T(8,128)S(1)} collective-permute-done((f32[136,128]{0,1:T(8,128)S(1)}, f32[136,128]{0,1:T(8,128)S(1)}, u32[]{:S(2)}, u32[]{:S(2)}) %collective-permute-start.14) | collective-permute-done | bytes 69664 | tf_op jit(solution)/shard_map/ppermute | solution.py:21
  366.8 3.2 collective-permute-start.22
  370.0 8.6 %collective-permute-done.21 = f32[392,128]{1,0:T(8,128)S(1)} collective-permute-done((f32[392,128]{1,0:T(8,128)S(1)}, f32[392,128]{1,0:T(8,128)S(1)}, u32[]{:S(2)}, u32[]{:S(2)}) %collective-permute-start.21) | collective-permute-done | bytes 200736 | tf_op jit(solution)/shard_map/ppermute | solution.py:21
  388.3 6.4 %combine.3 = bf16[384,512]{1,0:T(8,128)(2,1)S(1)} custom-call(bf16[128,48,512]{2,1,0:T(8,128)(2,1)} %all-to-all-done.3.returned, f32[3,128,128]{2,1,0:T(8,128)S(1)} %copy-done.18, f32[3,128,128]{2,1,0:T(8,128)S(1)} %copy-done.11, f32[384,512]{1,0:T(8,128)S(1)} %get-tuple-element.32.hidden), custom_call_target="tpu_custom_call" | custom-call | flops 805306368 | bytes 6291456 | tf_op jit(solution)/shard_map/combine/pallas_call | solution.py:268
  396.4 2.3 collective-permute-start.25
  399.9 2.4 collective-permute-done.24.left
  402.2 2.9 collective-permute-done.26.opposite
  (159 shorter events, 57.6 us)
Async XLA Ops:
  0.0 22.5 %collective-permute-start = (bf16[128,1280]{1,0:T(8,128)(2,1)}, bf16[128,1280]{1,0:T(8,128)(2,1)}, u32[]{:S(2)}, u32[]{:S(2)}) collective-permute-start(bf16[128,1280]{1,0:T(8,128)(2,1)} %param.17), channel_id=1, source_target_pairs={{0,1},{1,2},{2,3},{3,0},{4,5},{5,6},{6,7},{7,4},{8,9},{9,10},{10,1... | collective-permute-start | bytes 983048 | tf_op jit(solution)/shard_map/ppermute | solution.py:21
  2.0 22.2 %collective-permute-start.1 = (bf16[128,1280]{1,0:T(8,128)(2,1)}, bf16[128,1280]{1,0:T(8,128)(2,1)}, u32[]{:S(2)}, u32[]{:S(2)}) collective-permute-start(bf16[128,1280]{1,0:T(8,128)(2,1)} %param.17), channel_id=1, source_target_pairs={{0,3},{1,0},{2,1},{3,2},{4,7},{5,4},{6,5},{7,6},{8,11},{9,8},{10,9... | collective-permute-start | bytes 983048 | tf_op jit(solution)/shard_map/ppermute | solution.py:21
  4.2 21.8 %collective-permute-start.2 = (bf16[128,1280]{1,0:T(8,128)(2,1)}, bf16[128,1280]{1,0:T(8,128)(2,1)S(1)}, u32[]{:S(2)}, u32[]{:S(2)}) collective-permute-start(bf16[128,1280]{1,0:T(8,128)(2,1)} %param.17), channel_id=1, source_target_pairs={{0,2},{1,3},{2,0},{3,1},{4,6},{5,7},{6,4},{7,5},{8,10},{9,11},{10,... | collective-permute-start | bytes 983048 | tf_op jit(solution)/shard_map/ppermute | solution.py:21
  6.7 104.2 %copy-start.19 = (s32[4]{0:T(128)}, s32[4]{0:T(128)S(1)}, u32[]{:S(2)}) copy-start(s32[4]{0:T(128)S(1)} %compare_select_fusion.refs_0_.order) | copy-start | bytes 52
  10.7 11.2 %collective-permute-start.9 = (bf16[128,128]{1,0:T(8,128)(2,1)}, bf16[128,128]{1,0:T(8,128)(2,1)S(1)}, u32[]{:S(2)}, u32[]{:S(2)}) collective-permute-start(bf16[128,128]{1,0:T(8,128)(2,1)} %get-tuple-element.47), channel_id=1, source_target_pairs={{0,1},{1,2},{2,3},{3,0},{4,5},{5,6},{6,7},{7,4},{8,9},{9,10},{10,1... | collective-permute-start | bytes 98312 | tf_op jit(solution)/shard_map/ppermute | solution.py:21
  11.7 23.1 %collective-permute-start.10 = (bf16[128,128]{1,0:T(8,128)(2,1)}, bf16[128,128]{1,0:T(8,128)(2,1)S(1)}, u32[]{:S(2)}, u32[]{:S(2)}) collective-permute-start(bf16[128,128]{1,0:T(8,128)(2,1)} %get-tuple-element.47), channel_id=1, source_target_pairs={{0,3},{1,0},{2,1},{3,2},{4,7},{5,4},{6,5},{7,6},{8,11},{9,8},{10,9... | collective-permute-start | bytes 98312 | tf_op jit(solution)/shard_map/ppermute | solution.py:21
  21.9 28.7 %collective-permute-start.11 = (bf16[128,128]{1,0:T(8,128)(2,1)}, bf16[128,128]{1,0:T(8,128)(2,1)S(1)}, u32[]{:S(2)}, u32[]{:S(2)}) collective-permute-start(bf16[128,128]{1,0:T(8,128)(2,1)} %get-tuple-element.47), channel_id=1, source_target_pairs={{0,2},{1,3},{2,0},{3,1},{4,6},{5,7},{6,4},{7,5},{8,10},{9,11},{10,... | collective-permute-start | bytes 98312 | tf_op jit(solution)/shard_map/ppermute | solution.py:21
  29.8 7.1 %collective-permute-start.3 = (bf16[128,512]{1,0:T(8,128)(2,1)S(1)}, bf16[128,512]{1,0:T(8,128)(2,1)S(1)}, u32[]{:S(2)}, u32[]{:S(2)}) collective-permute-start(bf16[128,512]{1,0:T(8,128)(2,1)S(1)} %slice.56.refs_1_.columns), channel_id=1, source_target_pairs={{0,1},{1,2},{2,3},{3,0},{4,5},{5,6},{6,7},{7,4},{8,9},{9,10},{10,1... | collective-permute-start | bytes 393224 | tf_op jit(solution)/shard_map/ppermute | solution.py:21
  30.1 6.8 %collective-permute-start.4 = (bf16[128,512]{1,0:T(8,128)(2,1)S(1)}, bf16[128,512]{1,0:T(8,128)(2,1)S(1)}, u32[]{:S(2)}, u32[]{:S(2)}) collective-permute-start(bf16[128,512]{1,0:T(8,128)(2,1)S(1)} %slice.56.refs_1_.columns), channel_id=1, source_target_pairs={{0,3},{1,0},{2,1},{3,2},{4,7},{5,4},{6,5},{7,6},{8,11},{9,8},{10,9... | collective-permute-start | bytes 393224 | tf_op jit(solution)/shard_map/ppermute | solution.py:21
  33.0 6.5 %collective-permute-start.5 = (bf16[128,512]{1,0:T(8,128)(2,1)S(1)}, bf16[128,512]{1,0:T(8,128)(2,1)S(1)}, u32[]{:S(2)}, u32[]{:S(2)}) collective-permute-start(bf16[128,512]{1,0:T(8,128)(2,1)S(1)} %slice.56.refs_1_.columns), channel_id=1, source_target_pairs={{0,2},{1,3},{2,0},{3,1},{4,6},{5,7},{6,4},{7,5},{8,10},{9,11},{10,... | collective-permute-start | bytes 393224 | tf_op jit(solution)/shard_map/ppermute | solution.py:21
  46.7 7.6 %collective-permute-start.6 = (bf16[128,512]{1,0:T(8,128)(2,1)S(1)}, bf16[128,512]{1,0:T(8,128)(2,1)S(1)}, u32[]{:S(2)}, u32[]{:S(2)}) collective-permute-start(bf16[128,512]{1,0:T(8,128)(2,1)S(1)} %get-tuple-element.19), channel_id=1, source_target_pairs={{0,1},{1,2},{2,3},{3,0},{4,5},{5,6},{6,7},{7,4},{8,9},{9,10},{10,1... | collective-permute-start | bytes 393224 | tf_op jit(solution)/shard_map/ppermute | solution.py:21
  46.8 7.5 %collective-permute-start.7 = (bf16[128,512]{1,0:T(8,128)(2,1)S(1)}, bf16[128,512]{1,0:T(8,128)(2,1)S(1)}, u32[]{:S(2)}, u32[]{:S(2)}) collective-permute-start(bf16[128,512]{1,0:T(8,128)(2,1)S(1)} %get-tuple-element.20), channel_id=1, source_target_pairs={{0,3},{1,0},{2,1},{3,2},{4,7},{5,4},{6,5},{7,6},{8,11},{9,8},{10,9... | collective-permute-start | bytes 393224 | tf_op jit(solution)/shard_map/ppermute | solution.py:21
  50.0 6.5 %collective-permute-start.8 = (bf16[128,512]{1,0:T(8,128)(2,1)S(1)}, bf16[128,512]{1,0:T(8,128)(2,1)S(1)}, u32[]{:S(2)}, u32[]{:S(2)}) collective-permute-start(bf16[128,512]{1,0:T(8,128)(2,1)S(1)} %get-tuple-element.21), channel_id=1, source_target_pairs={{0,2},{1,3},{2,0},{3,1},{4,6},{5,7},{6,4},{7,5},{8,10},{9,11},{10,... | collective-permute-start | bytes 393224 | tf_op jit(solution)/shard_map/ppermute | solution.py:21
  59.7 94.5 %all-to-all-start = ((bf16[128,16,512]{2,1,0:T(8,128)(2,1)}), bf16[128,16,512]{2,1,0:T(8,128)(2,1)S(1)}, u32[]{:S(2)}, u32[]{:S(2)}) async-start(bf16[128,16,512]{2,1,0:T(8,128)(2,1)} %copy-done.2), calls=%async_computation | async-start | bytes 4194304 | tf_op jit(solution)/shard_map/all_to_all | solution.py:376
  68.9 33.3 %collective-permute-start.15 = (bf16[384,512]{1,0:T(8,128)(2,1)S(1)}, bf16[384,512]{1,0:T(8,128)(2,1)S(1)}, u32[]{:S(2)}, u32[]{:S(2)}) collective-permute-start(bf16[384,512]{1,0:T(8,128)(2,1)S(1)} %slice.60.refs_1_.columns), channel_id=1, source_target_pairs={{0,1},{1,2},{2,3},{3,0},{4,5},{5,6},{6,7},{7,4},{8,9},{9,10},{10,1... | collective-permute-start | bytes 1179656 | tf_op jit(solution)/shard_map/ppermute | solution.py:21
  70.0 32.1 %collective-permute-start.16 = (bf16[384,512]{1,0:T(8,128)(2,1)S(1)}, bf16[384,512]{1,0:T(8,128)(2,1)S(1)}, u32[]{:S(2)}, u32[]{:S(2)}) collective-permute-start(bf16[384,512]{1,0:T(8,128)(2,1)S(1)} %slice.60.refs_1_.columns), channel_id=1, source_target_pairs={{0,3},{1,0},{2,1},{3,2},{4,7},{5,4},{6,5},{7,6},{8,11},{9,8},{10,9... | collective-permute-start | bytes 1179656 | tf_op jit(solution)/shard_map/ppermute | solution.py:21
  72.2 38.7 %collective-permute-start.17 = (bf16[384,512]{1,0:T(8,128)(2,1)S(1)}, bf16[384,512]{1,0:T(8,128)(2,1)S(1)}, u32[]{:S(2)}, u32[]{:S(2)}) collective-permute-start(bf16[384,512]{1,0:T(8,128)(2,1)S(1)} %slice.60.refs_1_.columns), channel_id=1, source_target_pairs={{0,2},{1,3},{2,0},{3,1},{4,6},{5,7},{6,4},{7,5},{8,10},{9,11},{10,... | collective-permute-start | bytes 1179656 | tf_op jit(solution)/shard_map/ppermute | solution.py:21
  127.6 20.8 %collective-permute-start.18 = (bf16[384,512]{1,0:T(8,128)(2,1)S(1)}, bf16[384,512]{1,0:T(8,128)(2,1)S(1)}, u32[]{:S(2)}, u32[]{:S(2)}) collective-permute-start(bf16[384,512]{1,0:T(8,128)(2,1)S(1)} %get-tuple-element.27), channel_id=1, source_target_pairs={{0,1},{1,2},{2,3},{3,0},{4,5},{5,6},{6,7},{7,4},{8,9},{9,10},{10,1... | collective-permute-start | bytes 1179656 | tf_op jit(solution)/shard_map/ppermute | solution.py:21
  128.6 19.8 %collective-permute-start.19 = (bf16[384,512]{1,0:T(8,128)(2,1)S(1)}, bf16[384,512]{1,0:T(8,128)(2,1)S(1)}, u32[]{:S(2)}, u32[]{:S(2)}) collective-permute-start(bf16[384,512]{1,0:T(8,128)(2,1)S(1)} %get-tuple-element.28), channel_id=1, source_target_pairs={{0,3},{1,0},{2,1},{3,2},{4,7},{5,4},{6,5},{7,6},{8,11},{9,8},{10,9... | collective-permute-start | bytes 1179656 | tf_op jit(solution)/shard_map/ppermute | solution.py:21
  131.0 17.5 %collective-permute-start.20 = (bf16[384,512]{1,0:T(8,128)(2,1)S(1)}, bf16[384,512]{1,0:T(8,128)(2,1)S(1)}, u32[]{:S(2)}, u32[]{:S(2)}) collective-permute-start(bf16[384,512]{1,0:T(8,128)(2,1)S(1)} %get-tuple-element.29), channel_id=1, source_target_pairs={{0,2},{1,3},{2,0},{3,1},{4,6},{5,7},{6,4},{7,5},{8,10},{9,11},{10,... | collective-permute-start | bytes 1179656 | tf_op jit(solution)/shard_map/ppermute | solution.py:21
  154.2 89.3 %all-to-all-start.2 = ((bf16[128,48,512]{2,1,0:T(8,128)(2,1)}), bf16[128,48,512]{2,1,0:T(8,128)(2,1)}, u32[]{:S(2)}, u32[]{:S(2)}) async-start(bf16[128,48,512]{2,1,0:T(8,128)(2,1)} %get-tuple-element.31), calls=%async_computation.2 | async-start | bytes 12582912 | tf_op jit(solution)/shard_map/all_to_all | solution.py:376
  243.6 38.2 %all-to-all-start.1 = ((bf16[128,16,512]{2,1,0:T(8,128)(2,1)}), bf16[128,16,512]{2,1,0:T(8,128)(2,1)S(1)}, u32[]{:S(2)}, u32[]{:S(2)}) async-start(bf16[128,16,512]{2,1,0:T(8,128)(2,1)} %bitcast.79), calls=%async_computation.1 | async-start | bytes 4194304 | tf_op jit(solution)/shard_map/all_to_all | solution.py:386
  281.8 104.7 %all-to-all-start.3 = ((bf16[128,48,512]{2,1,0:T(8,128)(2,1)}), bf16[128,48,512]{2,1,0:T(8,128)(2,1)}, u32[]{:S(2)}, u32[]{:S(2)}) async-start(bf16[128,48,512]{2,1,0:T(8,128)(2,1)} %bitcast.87), calls=%async_computation.3 | async-start | bytes 12582912 | tf_op jit(solution)/shard_map/all_to_all | solution.py:386
  289.2 69.1 %collective-permute-start.12 = (f32[136,128]{0,1:T(8,128)S(1)}, f32[136,128]{0,1:T(8,128)S(1)}, u32[]{:S(2)}, u32[]{:S(2)}) collective-permute-start(f32[136,128]{0,1:T(8,128)S(1)} %select_maximum_fusion.1), channel_id=1, source_target_pairs={{0,1},{1,2},{2,3},{3,0},{4,5},{5,6},{6,7},{7,4},{8,9},{9,10},{10,1... | collective-permute-start | bytes 208904 | tf_op jit(solution)/shard_map/ppermute | solution.py:21
  290.3 68.1 %collective-permute-start.13 = (f32[136,128]{0,1:T(8,128)S(1)}, f32[136,128]{0,1:T(8,128)S(1)}, u32[]{:S(2)}, u32[]{:S(2)}) collective-permute-start(f32[136,128]{0,1:T(8,128)S(1)} %select_maximum_fusion.1), channel_id=1, source_target_pairs={{0,3},{1,0},{2,1},{3,2},{4,7},{5,4},{6,5},{7,6},{8,11},{9,8},{10,9... | collective-permute-start | bytes 208904 | tf_op jit(solution)/shard_map/ppermute | solution.py:21
  292.5 72.6 %collective-permute-start.14 = (f32[136,128]{0,1:T(8,128)S(1)}, f32[136,128]{0,1:T(8,128)S(1)}, u32[]{:S(2)}, u32[]{:S(2)}) collective-permute-start(f32[136,128]{0,1:T(8,128)S(1)} %select_maximum_fusion.1), channel_id=1, source_target_pairs={{0,2},{1,3},{2,0},{3,1},{4,6},{5,7},{6,4},{7,5},{8,10},{9,11},{10,... | collective-permute-start | bytes 208904 | tf_op jit(solution)/shard_map/ppermute | solution.py:21
  366.7 12.0 %collective-permute-start.21 = (f32[392,128]{1,0:T(8,128)S(1)}, f32[392,128]{1,0:T(8,128)S(1)}, u32[]{:S(2)}, u32[]{:S(2)}) collective-permute-start(f32[392,128]{1,0:T(8,128)S(1)} %select_maximum_fusion), channel_id=1, source_target_pairs={{0,1},{1,2},{2,3},{3,0},{4,5},{5,6},{6,7},{7,4},{8,9},{9,10},{10,1... | collective-permute-start | bytes 602120 | tf_op jit(solution)/shard_map/ppermute | solution.py:21
  366.8 11.9 %collective-permute-start.22 = (f32[392,128]{1,0:T(8,128)S(1)}, f32[392,128]{1,0:T(8,128)S(1)}, u32[]{:S(2)}, u32[]{:S(2)}) collective-permute-start(f32[392,128]{1,0:T(8,128)S(1)} %select_maximum_fusion), channel_id=1, source_target_pairs={{0,3},{1,0},{2,1},{3,2},{4,7},{5,4},{6,5},{7,6},{8,11},{9,8},{10,9... | collective-permute-start | bytes 602120 | tf_op jit(solution)/shard_map/ppermute | solution.py:21
  370.0 8.7 %collective-permute-start.23 = (f32[392,128]{1,0:T(8,128)S(1)}, f32[392,128]{1,0:T(8,128)S(1)}, u32[]{:S(2)}, u32[]{:S(2)}) collective-permute-start(f32[392,128]{1,0:T(8,128)S(1)} %select_maximum_fusion), channel_id=1, source_target_pairs={{0,2},{1,3},{2,0},{3,1},{4,6},{5,7},{6,4},{7,5},{8,10},{9,11},{10,... | collective-permute-start | bytes 602120 | tf_op jit(solution)/shard_map/ppermute | solution.py:21
  395.5 6.8 %collective-permute-start.24 = (bf16[128,512]{1,0:T(8,128)(2,1)S(1)}, bf16[128,512]{1,0:T(8,128)(2,1)S(1)}, u32[]{:S(2)}, u32[]{:S(2)}) collective-permute-start(bf16[128,512]{1,0:T(8,128)(2,1)S(1)} %get-tuple-element.37), channel_id=1, source_target_pairs={{0,1},{1,2},{2,3},{3,0},{4,5},{5,6},{6,7},{7,4},{8,9},{9,10},{10,1... | collective-permute-start | bytes 393224 | tf_op jit(solution)/shard_map/ppermute | solution.py:21
  396.4 5.9 %collective-permute-start.25 = (bf16[128,512]{1,0:T(8,128)(2,1)S(1)}, bf16[128,512]{1,0:T(8,128)(2,1)S(1)}, u32[]{:S(2)}, u32[]{:S(2)}) collective-permute-start(bf16[128,512]{1,0:T(8,128)(2,1)S(1)} %get-tuple-element.36), channel_id=1, source_target_pairs={{0,3},{1,0},{2,1},{3,2},{4,7},{5,4},{6,5},{7,6},{8,11},{9,8},{10,9... | collective-permute-start | bytes 393224 | tf_op jit(solution)/shard_map/ppermute | solution.py:21
  398.7 6.5 %collective-permute-start.26 = (bf16[128,512]{1,0:T(8,128)(2,1)S(1)}, bf16[128,512]{1,0:T(8,128)(2,1)S(1)}, u32[]{:S(2)}, u32[]{:S(2)}) collective-permute-start(bf16[128,512]{1,0:T(8,128)(2,1)S(1)} %get-tuple-element.35), channel_id=1, source_target_pairs={{0,2},{1,3},{2,0},{3,1},{4,6},{5,7},{6,4},{7,5},{8,10},{9,11},{10,... | collective-permute-start | bytes 393224 | tf_op jit(solution)/shard_map/ppermute | solution.py:21
  (36 other events, 469.0 us)

commit v2 on v1

v2 whole, which is shorter than its diff:
```python
import math

import jax
import jax.numpy as jnp
from jax import lax
from jax.experimental import pallas as pl
from jax.experimental.pallas import tpu as pltpu
from jax.sharding import PartitionSpec as P

EPSILON = 1e-06
ROPE_BASE = 1000000.0
F32 = jnp.float32
BF16 = jnp.bfloat16
VMEM_BYTES = 32 * 1024 * 1024
EXPERT_VMEM_BYTES = 56 * 1024 * 1024


def whole(count):
    return [pl.BlockSpec(memory_space=pltpu.VMEM)] * count


def far(count):
    return [pl.BlockSpec(memory_space=pltpu.HBM)] * count


def in_far(values):
    return [pltpu.with_memory_space_constraint(value, pltpu.HBM) for value in values]


def shift(value, by):
    size = lax.axis_size("tp")
    return lax.ppermute(value, "tp", [(i, (i + by) % size) for i in range(size)])


def rope_tables(seq_len, head_dim):
    half_dim = head_dim // 2
    inv_freq = ROPE_BASE ** (-(jnp.arange(half_dim, dtype=F32) * 2.0) / head_dim)
    angles = jnp.arange(seq_len, dtype=F32)[:, None] * inv_freq[None, :]
    cos, sin = jnp.cos(angles), jnp.sin(angles)
    return jnp.concatenate([cos, cos], axis=1), jnp.concatenate([-sin, sin], axis=1)


def columns_kernel(order, own, left, right, opposite, weight, bias, extra, first, second, near, sems):
    sources = (own, left, right, opposite)
    rows = own.shape[0]
    some = second.shape[0] // rows
    copies = [
        pltpu.make_async_copy(source, near.at[place], sems.at[place])
        for place, source in enumerate(sources)
    ]
    for copy in copies:
        copy.start()
    first[pl.ds(some * rows, extra.shape[0]), :] = extra[...]
    part = bias[pl.ds(order[0], 1), :]
    for place, copy in enumerate(copies):
        copy.wait()
        product = jnp.dot(near[place], weight[...], preferred_element_type=F32)
        product = (product + part).astype(BF16)
        at = order[place]
        for number in range(2 * some):
            out = (first, second)[number // some]

            @pl.when(at == number)
            def _():
                out[pl.ds(number % some * rows, rows), :] = product


def run_columns(order, pieces, weight, bias, extra):
    rows, depth = pieces[0].shape
    width = weight.shape[1]
    half = jax.ShapeDtypeStruct((2 * rows, width), BF16)
    longer = jax.ShapeDtypeStruct((2 * rows + extra.shape[0], width), BF16)
    return pl.pallas_call(
        columns_kernel,
        in_specs=[pl.BlockSpec(memory_space=pltpu.SMEM)] + far(4) + whole(3),
        out_specs=whole(2),
        out_shape=(longer, half),
        scratch_shapes=[pltpu.VMEM((4, rows, depth), BF16), pltpu.SemaphoreType.DMA((4,))],
        compiler_params=pltpu.CompilerParams(vmem_limit_bytes=VMEM_BYTES),
        cost_estimate=pl.CostEstimate(
            flops=8 * rows * weight.size, transcendentals=0,
            bytes_accessed=2 * weight.size + 8 * pieces[0].size,
        ),
        name="columns",
    )(order, *in_far(pieces), weight, bias, extra)


def chosen_kernel(order, own, left, right, opposite, first, second):
    experts, blocks, cap, columns = first.shape
    tokens = columns // blocks
    some = own.shape[0]
    slot = lax.broadcasted_iota(jnp.int32, (some, cap, tokens), 1).astype(F32)
    for place, piece in enumerate((own, left, right, opposite)):
        at = order[place]
        for number in range(2 * blocks):
            out = (first, second)[number // blocks]
            block = number % blocks

            @pl.when(at == number)
            def _():
                for part in range(experts // some):
                    places = piece[:, pl.ds(part * tokens, tokens)].astype(F32)
                    here = pl.ds(part * some, some)
                    met = jnp.broadcast_to(places[:, None, :], slot.shape) == slot
                    met = met.astype(F32).astype(BF16)
                    for other in range(blocks):
                        out[here, block, :, pl.ds(other * tokens, tokens)] = (
                            met if other == block else jnp.zeros_like(met)
                        )


def run_chosen(order, parts, tokens, experts, cap):
    rows, width = parts[0].shape
    some = experts * tokens // width
    table = pl.BlockSpec((some, width), lambda i: (rows // some - 1, 0))
    half = (experts, 2, cap, 2 * tokens)
    result = pl.BlockSpec(half, lambda i: (0, 0, 0, 0))
    return pl.pallas_call(
        chosen_kernel,
        grid=(1,),
        in_specs=[pl.BlockSpec(memory_space=pltpu.SMEM)] + [table] * 4,
        out_specs=[result] * 2,
        out_shape=(jax.ShapeDtypeStruct(half, BF16),) * 2,
        compiler_params=pltpu.CompilerParams(vmem_limit_bytes=VMEM_BYTES),
        name="chosen",
    )(order, *parts)


def layer_kernel(*refs, first):
    order, sources, refs = refs[0], refs[1:5], refs[5:]
    if first:
        past_keys, past_values = refs[:2]
        refs = refs[2:]
    weights, refs = refs[:4], refs[4:]
    (gain, q_gain, k_gain, cos, sin, seg_col, seg_row,
     to_right, to_left, to_opposite, to_own, keys_out, values_out,
     normed, queries, keys, values, context, near, w_k, w_v, w_q, w_o, sems) = refs
    count, width = to_own.shape
    feat_dim = w_q.shape[0]
    head_dim = w_k.shape[1]
    heads = queries.shape[0]
    block = 128
    factor = float(head_dim) ** -0.5 * math.log2(math.e)

    copies = [
        pltpu.make_async_copy(source.at[pl.ds(0, count), :], near.at[place], sems.at[place])
        for place, source in enumerate(sources)
    ] + [
        pltpu.make_async_copy(source, target, sems.at[4 + place])
        for place, (source, target) in enumerate(zip(weights, (w_k, w_v, w_q, w_o)))
    ]
    for copy in copies:
        copy.start()
    for copy in copies[:4]:
        copy.wait()

    pieces = [near[place].astype(F32) for place in range(4)]
    squares = sum(jnp.sum(piece * piece, axis=1, keepdims=True) for piece in pieces)
    scale = lax.rsqrt(squares / feat_dim + EPSILON)
    for place, piece in enumerate(pieces):
        at = order[place]
        columns = pl.ds(pl.multiple_of(at * width, width), width)
        normed[:, columns] = (piece * scale * gain[pl.ds(at, 1), :]).astype(BF16)

    here = pl.ds(first, count)
    turn_cos, turn_sin = cos[here, :], sin[here, :]

    def head_of(raw, head_gain):
        squares = jnp.mean(raw * raw, axis=1, keepdims=True)
        raw = raw * lax.rsqrt(squares + EPSILON) * head_gain[...]
        return (raw * turn_cos + pltpu.roll(raw, head_dim // 2, 1) * turn_sin).astype(BF16)

    if first:
        keys[:first, :] = past_keys[...]
        values[:first, :] = past_values[...]
    copies[4].wait()
    new_keys = head_of(jnp.dot(normed[...], w_k[...], preferred_element_type=F32), k_gain)
    copies[5].wait()
    new_values = jnp.dot(normed[...], w_v[...], preferred_element_type=F32).astype(BF16)
    keys[here, :] = new_keys
    values[here, :] = new_values
    keys_out[...] = new_keys
    values_out[...] = new_values
    copies[6].wait()
    for pair in range(heads // 2):
        raw = jnp.dot(
            normed[...], w_q[:, pl.ds(pair * 2 * head_dim, 2 * head_dim)],
            preferred_element_type=F32,
        )
        for one in range(2):
            queries[2 * pair + one] = head_of(raw[:, one * head_dim : (one + 1) * head_dim], q_gain)

    for start in range(0, count, block):
        span = first + start + block
        row_at = first + start + lax.broadcasted_iota(jnp.int32, (block, span), 0)
        col_at = lax.broadcasted_iota(jnp.int32, (block, span), 1)
        same = seg_col[pl.ds(first + start, block), :] == seg_row[:, :span]
        allowed = same & (col_at <= row_at)
        for head in range(heads):
            scores = lax.dot_general(
                queries[head, pl.ds(start, block), :], keys[:span, :], (((1,), (1,)), ((), ())),
                preferred_element_type=F32,
            )
            scores = jnp.where(allowed, scores, -1e30)
            expo = jnp.exp2((scores - jnp.max(scores, axis=1, keepdims=True)) * factor)
            total = jnp.sum(expo, axis=1, keepdims=True)
            mixed = jnp.dot(expo.astype(BF16), values[:span, :], preferred_element_type=F32)
            context[pl.ds(start, block), pl.ds(head * head_dim, head_dim)] = (
                mixed / total
            ).astype(BF16)

    copies[7].wait()
    for place, out in ((2, to_right), (1, to_left), (3, to_opposite), (0, to_own)):
        columns = pl.ds(pl.multiple_of(order[place] * width, width), width)
        out[...] = jnp.dot(context[...], w_o[:, columns], preferred_element_type=F32).astype(BF16)


def run_layer(
    order, parts, count, past, first, gain, w_q, w_k, w_v, w_o, q_gain, k_gain, cos, sin, seg
):
    width = parts[0].shape[1]
    feat_dim = w_q.shape[0]
    head_dim = w_k.shape[1]
    heads = w_q.shape[1] // head_dim
    span = first + count
    piece = jax.ShapeDtypeStruct((count, width), BF16)
    kv = jax.ShapeDtypeStruct((count, head_dim), BF16)
    weights = (w_k, w_v, w_q, w_o)
    operands = [*in_far(parts), *past, *in_far(weights), gain, q_gain, k_gain, cos, sin, *seg]

    def kernel(*refs):
        layer_kernel(*refs, first=first)

    return pl.pallas_call(
        kernel,
        in_specs=[pl.BlockSpec(memory_space=pltpu.SMEM)]
        + far(len(parts)) + whole(len(past)) + far(len(weights))
        + whole(len(operands) - len(parts) - len(past) - len(weights)),
        out_specs=whole(6),
        out_shape=(piece,) * 4 + (kv,) * 2,
        scratch_shapes=[
            pltpu.VMEM((count, feat_dim), BF16),
            pltpu.VMEM((heads, count, head_dim), BF16),
            pltpu.VMEM((span, head_dim), BF16),
            pltpu.VMEM((span, head_dim), BF16),
            pltpu.VMEM((count, heads * head_dim), BF16),
            pltpu.VMEM((len(parts), count, width), BF16),
        ]
        + [pltpu.VMEM(weight.shape, BF16) for weight in weights]
        + [pltpu.SemaphoreType.DMA((len(parts) + len(weights),))],
        compiler_params=pltpu.CompilerParams(vmem_limit_bytes=VMEM_BYTES),
        cost_estimate=pl.CostEstimate(
            flops=4 * count * feat_dim * (heads + 1) * head_dim
            + 4 * count * span * heads * head_dim,
            transcendentals=count * span * heads,
            bytes_accessed=4 * feat_dim * (heads + 1) * head_dim + 16 * count * width,
        ),
        name="layer",
    )(order, *operands)


def expert_kernel(rows, gain, w_gate_up, w_down, *rest):
    out, normed = rest[-2:]
    groups, parts, slots, width = rows.shape
    count = groups * slots
    feat_dim = parts * width
    inner = w_down.shape[0]
    pieces = [rows[:, part].reshape(count, width).astype(F32) for part in range(parts)]
    squares = sum(jnp.sum(piece * piece, axis=1, keepdims=True) for piece in pieces)
    scale = lax.rsqrt(squares / feat_dim + EPSILON)
    for part, piece in enumerate(pieces):
        normed[:, pl.ds(part * width, width)] = (
            piece * scale * gain[pl.ds(part, 1), :]
        ).astype(BF16)
    both = jnp.dot(normed[...], w_gate_up[...], preferred_element_type=F32)
    gate, up = both[:, :inner], both[:, inner:]
    hidden = (gate * jax.nn.sigmoid(gate) * up).astype(BF16)
    result = jnp.dot(hidden, w_down[...], preferred_element_type=F32)
    out[...] = result.astype(BF16).reshape(out.shape)


def run_experts(arrived, gain, w_gate_up, w_down, cap, chunk, earlier):
    sources, parts, slots, width = arrived.shape
    feat_dim, double = w_gate_up.shape
    groups = 8
    blocks = slots // cap

    def fixed(shape):
        return pl.BlockSpec(shape, lambda i: (0, 0), pipeline_mode=pl.Buffered(1))

    more = () if earlier is None else (earlier,)
    return pl.pallas_call(
        expert_kernel,
        grid=(sources // groups,),
        in_specs=[
            pl.BlockSpec((groups, parts, slots, width), lambda i: (i, 0, 0, 0)),
            fixed(gain.shape), fixed(w_gate_up.shape), fixed(w_down.shape),
        ] + [pl.BlockSpec(memory_space=pl.ANY)] * len(more),
        out_specs=pl.BlockSpec((groups, blocks, cap, feat_dim), lambda i: (i, chunk, 0, 0)),
        out_shape=pltpu.HBM((sources, parts, cap, feat_dim), BF16),
        scratch_shapes=[pltpu.VMEM((groups * slots, feat_dim), BF16)],
        input_output_aliases={4: 0} if more else {},
        compiler_params=pltpu.CompilerParams(vmem_limit_bytes=EXPERT_VMEM_BYTES),
        cost_estimate=pl.CostEstimate(
            flops=3 * sources * slots * feat_dim * double,
            transcendentals=sources * slots * double // 2,
            bytes_accessed=4 * sources * slots * feat_dim + 3 * feat_dim * double,
        ),
        name="experts",
    )(*in_far([arrived]), gain, *in_far([w_gate_up, w_down]), *more)


def join_kernel(order, own, left, right, opposite, out):
    width = own.shape[1]
    for place, piece in enumerate((own, left, right, opposite)):
        out[:, pl.ds(pl.multiple_of(order[place] * width, width), width)] = piece[...]


def run_join(order, pieces):
    count, width = pieces[0].shape
    return pl.pallas_call(
        join_kernel,
        in_specs=[pl.BlockSpec(memory_space=pltpu.SMEM)] + whole(4),
        out_specs=whole(1)[0],
        out_shape=jax.ShapeDtypeStruct((count, 4 * width), BF16),
        name="join",
    )(order, *pieces)


def on_device(
    audio_feats, w_audio, b_audio, segments, w_q, w_k, w_v, w_o, attn_gain, q_gain, k_gain,
    moe_gain, w_router, routes, w_gate_up, w_down,
):
    me = lax.axis_index("tp")
    tp_size = lax.axis_size("tp")
    tok_rows = audio_feats.shape[0]
    feat_dim = b_audio.shape[0]
    seq_len = segments.shape[1]
    head_dim = q_gain.shape[0]
    experts = w_router.shape[1]
    top_count = routes.shape[1]
    width = w_audio.shape[1]
    slot_cap = max(4, 2 * tok_rows * top_count // experts)
    order = lax.rem(me + jnp.array([0, 3, 1, 2], jnp.int32), tp_size)

    def exchange(value):
        return [value, shift(value, 1), shift(value, -1), shift(value, 2)]

    def in_order(value):
        stack = jnp.zeros((tp_size,) + value.shape, value.dtype)
        for place, piece in enumerate(exchange(value)):
            stack = lax.dynamic_update_slice_in_dim(stack, piece[None], order[place], 0)
        return stack

    expert_ids = jnp.arange(experts, dtype=jnp.int32)
    named = jnp.any(routes[:, :, None] == expert_ids[None, None, :], axis=1)
    token_ids = jnp.arange(tok_rows, dtype=jnp.int32)
    earlier = (token_ids[None, :] < token_ids[:, None]).astype(BF16)
    my_places = jnp.dot(earlier, named.astype(BF16), preferred_element_type=F32)
    my_places = jnp.where(named, my_places, -1.0).astype(BF16)
    groups = width // tok_rows
    extra = my_places.T.reshape(groups, -1, tok_rows).transpose(1, 0, 2).reshape(-1, width)

    chunk_a, chunk_b = run_columns(
        order, exchange(audio_feats), w_audio, b_audio.reshape(tp_size, width), extra
    )
    parts_a = exchange(chunk_a)
    chunk_b, _ = lax.optimization_barrier((chunk_b, parts_a[1]))
    parts_b = exchange(chunk_b)

    cos, sin = rope_tables(seq_len, head_dim)
    seg = (segments.reshape(seq_len, 1), segments)
    by_device = (tp_size, width)
    half = seq_len // 2

    def layer(first, parts, past):
        *pieces, keys, values = run_layer(
            order, parts, half, past, first, attn_gain.reshape(by_device), w_q, w_k, w_v, w_o,
            q_gain[None], k_gain[None], cos, sin, seg,
        )
        return pieces, (keys, values)

    def summands(pieces):
        to_right, to_left, to_opposite, mine = pieces
        return [shift(to_right, 1), shift(to_left, -1), shift(to_opposite, 2), mine]

    pieces_a, past = layer(0, parts_a, ())
    pieces_b, _ = layer(half, parts_b, past)
    tables, pieces_b = lax.optimization_barrier((parts_a, pieces_b))
    met = run_chosen(order, tables, tok_rows, experts, slot_cap)
    terms = (summands(pieces_a), summands(pieces_b))

    sent = []
    for number, (chunk, term) in enumerate(zip((chunk_a[:half], chunk_b), terms)):
        hidden = sum(piece.astype(F32) for piece in term) + chunk.astype(F32)
        hidden = hidden.astype(BF16)
        rows = jnp.dot(met[number].reshape(-1, half), hidden, preferred_element_type=F32).astype(BF16)
        sent.append((rows.reshape(experts, -1, width), hidden))
    first_rows, _ = lax.optimization_barrier((sent[0][0], terms[1]))
    results = None
    for number, rows in enumerate((first_rows, sent[1][0])):
        arrived = lax.all_to_all(rows, ("exp", "tp"), 0, 0, tiled=True)
        results = run_experts(
            arrived.reshape(-1, tp_size, rows.shape[1], width), moe_gain.reshape(by_device),
            w_gate_up[0], w_down[0], slot_cap, number, results,
        )
        if number == 0:
            halves, results = lax.optimization_barrier(([rows for _, rows in sent], results))
    blocks = jnp.concatenate(halves, axis=0)
    blocks = blocks.reshape(tp_size, tok_rows, width)

    def block_of(place):
        return lax.dynamic_index_in_dim(blocks, order[place], 0, keepdims=False)

    own = [block_of(0), shift(block_of(2), 1), shift(block_of(1), -1), shift(block_of(3), 2)]
    results, own = lax.optimization_barrier((results, own))
    hidden_res = run_join(order, own)
    hidden_res = hidden_res.astype(F32)
    returned = lax.all_to_all(
        results.reshape(experts, slot_cap, feat_dim), ("exp", "tp"), 0, 0, tiled=True
    )
    squares = jnp.mean(hidden_res * hidden_res, axis=-1, keepdims=True)
    normed = (hidden_res * lax.rsqrt(squares + EPSILON) * moe_gain).astype(BF16)

    logits = jnp.dot(normed, w_router, preferred_element_type=F32)
    peak = jnp.max(jnp.where(named, logits, -jnp.inf), axis=1, keepdims=True)
    expo = jnp.where(named, jnp.exp(jnp.minimum(logits - peak, 0.0)), 0.0)
    gates = (expo / jnp.sum(expo, axis=1, keepdims=True)).astype(BF16)
    slot_of = jnp.arange(experts * slot_cap, dtype=jnp.int32)
    spread = (expert_ids[:, None] == (slot_of // slot_cap)[None, :]).astype(BF16)
    wide_gates = jnp.dot(gates, spread, preferred_element_type=F32)
    wide_places = jnp.dot(my_places, spread, preferred_element_type=F32)
    combine = jnp.where(
        wide_places == (slot_of % slot_cap).astype(F32)[None, :], wide_gates, 0.0
    ).astype(BF16)
    moe_out = jnp.dot(
        combine, returned.reshape(experts * slot_cap, feat_dim), preferred_element_type=F32
    )
    return (hidden_res + moe_out).astype(BF16)


def solution(mesh):
    in_specs = (
        P(("exp", "tp"), None),
        P(None, "tp"),
        P(),
        P("exp", None),
        P(None, "tp"),
        P(None, "tp"),
        P(None, "tp"),
        P("tp", None),
        P(),
        P(),
        P(),
        P(),
        P(),
        P(("exp", "tp"), None),
        P(("exp", "tp"), None, None),
        P(("exp", "tp"), None, None),
    )
    out_specs = P(("exp", "tp"), None)
    return jax.shard_map(
        on_device, mesh=mesh, in_specs=in_specs, out_specs=out_specs, check_vma=False
    )
```

time: 412 us -> 340 us (0.83)
  waiting for transfers between devices: 225 us -> 197 us
  starting transfers between devices: 71.3 us -> 47 us
  local copies, waits for them, and re-layouts: 21.8 us -> 9.48 us
  Pallas kernels: 70.2 us -> 59.1 us
  matrix products: 5.32 us -> 14.1 us
    ppermute x27 -> x18, waiting for transfers between devices: 150 us -> 25.6 us  [shift(): lax.ppermute(value, 'tp', [(i, (i + by) % size) for i in range(size)])]
    all_to_all x4 -> x3, waiting for transfers between devices: 75.4 us -> 171 us  [the longest x1 103 us: on_device(): lax.all_to_all(results.reshape(experts, slot_cap, feat_dim), ('exp', 'tp'...]
    ppermute x27 -> x18, starting transfers between devices: 39.6 us -> 26.3 us  [shift(): lax.ppermute(value, 'tp', [(i, (i + by) % size) for i in range(size)])]
    all_to_all x4 -> x3, starting transfers between devices: 31.7 us -> 20.7 us  [the longest x2 14.8 us: on_device(): arrived = lax.all_to_all(rows, ('exp', 'tp'), 0, 0, tiled=True)]
    pallas_call x6 -> x4, Pallas kernels: 47.2 us -> 37.3 us  [the longest x2 32.9 us: run_experts(): pl.pallas_call(expert_kernel, grid=(sources // groups,), in_specs=[pl.Blo...]
    dot_general x4 -> x6, matrix products: 5.32 us -> 14.1 us  [the longest x2 6.43 us: on_device(): jnp.dot(met[number].reshape(-1, half), hidden, preferred_element_type=F32)]
    unnamed x74 -> x64, local copies, waits for them, and re-layouts: 11.5 us -> 6.51 us
    dynamic_update_slice x7 -> x0, local copies, waits for them, and re-layouts: 4.26 us -> none  [in_order(): stack = lax.dynamic_update_slice_in_dim(stack, piece[None], order[place], 0)]
  transfers between devices with their start and end apart: 31 -> 21, of which waited for: 14 -> 9; matrix products, arithmetic and copies ran while one was open for 5% -> 5% of each run, Pallas kernels for 15% -> 17%
where the time goes in v2:
time: 340 us; the launch traced here: 339 us
  waiting for transfers between devices  197 us (58%)
  Pallas kernels  59.1 us (17%)
  starting transfers between devices  47 us (14%)
  matrix products  14.1 us (4%)
  local copies, waits for them, and re-layouts  9.48 us (3%)
  between operations  8.09 us (2%)
  other arithmetic  4.9 us (1%)
    all_to_all x1, waiting for transfers between devices, on_device(): lax.all_to_all(results.reshape(experts, slot_cap, feat_dim), ('exp', 'tp'...  103 us
    all_to_all x2, waiting for transfers between devices, on_device(): arrived = lax.all_to_all(rows, ('exp', 'tp'), 0, 0, tiled=True)  68.2 us
    pallas_call x2, Pallas kernels, run_experts(): pl.pallas_call(expert_kernel, grid=(sources // groups,), in_specs=[pl.Blo...  32.9 us
    ppermute x18, starting transfers between devices, shift(): lax.ppermute(value, 'tp', [(i, (i + by) % size) for i in range(size)])  26.3 us
    ppermute x18, waiting for transfers between devices, shift(): lax.ppermute(value, 'tp', [(i, (i + by) % size) for i in range(size)])  25.6 us
    pallas_call x2, Pallas kernels, run_layer(): pl.pallas_call(kernel, in_specs=[pl.BlockSpec(memory_space=pltpu.SMEM)] +...  19.8 us
    all_to_all x2, starting transfers between devices, on_device(): arrived = lax.all_to_all(rows, ('exp', 'tp'), 0, 0, tiled=True)  14.8 us
  transfers between devices with their start and end apart: 21, of which 9 were waited for; matrix products, arithmetic and copies ran while one was open for 5% of the time, Pallas kernels for 17%

profile of v2, /device:TPU:0, one launch (start us, length us, event | category | flops | bytes accessed | tf_op | source)
XLA Modules:
  0.0 339.4 jit_solution(18039990348530001834)
XLA Ops:
  0.0 2.1 collective-permute-start
  2.1 2.2 collective-permute-start.1
  4.3 1.8 collective-permute-start.2
  8.9 3.3 collective-permute-done.left
  12.1 6.5 %collective-permute-done.1.right = bf16[128,1280]{1,0:T(8,128)(2,1)S(1)} collective-permute-done((bf16[128,1280]{1,0:T(8,128)(2,1)}, bf16[128,1280]{1,0:T(8,128)(2,1)S(1)}, u32[]{:S(2)}, u32[]{:S(2)}) %collective-permute-start.1) | collective-permute-done | bytes 327712 | tf_op jit(solution)/shard_map/ppermute | solution.py:32
  18.6 1.7 collective-permute-done.2.opposite
  22.4 3.0 columns.1
  26.6 2.1 collective-permute-start.4
  30.0 10.3 %collective-permute-done.3.refs_2_.left = bf16[288,512]{1,0:T(8,128)(2,1)S(1)} collective-permute-done((bf16[288,512]{1,0:T(8,128)(2,1)S(1)}, bf16[288,512]{1,0:T(8,128)(2,1)S(1)}, u32[]{:S(2)}, u32[]{:S(2)}) %collective-permute-start.3) | collective-permute-done | bytes 294944 | tf_op jit(solution)/shard_map/ppermute | solution.py:32
  40.3 3.2 collective-permute-start.7
  44.8 8.8 %layer.2 = (bf16[256,512]{1,0:T(8,128)(2,1)S(1)}, bf16[256,512]{1,0:T(8,128)(2,1)S(1)}, bf16[256,512]{1,0:T(8,128)(2,1)S(1)}, bf16[256,512]{1,0:T(8,128)(2,1)S(1...) custom-call(s32[4]{0:T(128)S(1)} %compare_select_fusion.order.refs_0_, bf16[288,512]{1,0:T(8,128)(2,1)} %copy-done.1, ...), custom_call_target="tpu_custom_call" | custom-call | flops 2684354560 | bytes 11534336 | tf_op jit(solution)/shard_map/layer/pallas_call | solution.py:234
  54.6 2.4 collective-permute-start.13
  56.9 2.3 collective-permute-start.14
  60.0 11.0 %layer.3 = (bf16[256,512]{1,0:T(8,128)(2,1)S(1)}, bf16[256,512]{1,0:T(8,128)(2,1)S(1)}, bf16[256,512]{1,0:T(8,128)(2,1)S(1)}, bf16[256,512]{1,0:T(8,128)(2,1)S(1...) custom-call(s32[4]{0:T(128)S(1)} %compare_select_fusion.order.refs_0_, bf16[256,512]{1,0:T(8,128)(2,1)} %copy-done.10, ...), custom_call_target="tpu_custom_call" | custom-call | flops 2952790016 | bytes 11534336 | tf_op jit(solution)/shard_map/layer/pallas_call | solution.py:234
  72.6 1.4 chosen.1
  74.0 1.4 collective-permute-start.9
  75.6 3.2 convolution_convert_fusion
  79.8 2.7 collective-permute-done.9
  83.3 8.8 %all-to-all-start.1 = ((bf16[128,32,512]{2,1,0:T(8,128)(2,1)}), bf16[128,32,512]{2,1,0:T(8,128)(2,1)}, u32[]{:S(2)}, u32[]{:S(2)}) async-start(bf16[128,32,512]{2,1,0:T(8,128)(2,1)} %bitcast.51), calls=%async_computation.1 | async-start | bytes 8388608 | tf_op jit(solution)/shard_map/all_to_all | solution.py:402
  94.1 3.2 convolution_convert_fusion.1
  97.3 47.0 %all-to-all-done.1 = bf16[128,32,512]{2,1,0:T(8,128)(2,1)} async-done(((bf16[128,32,512]{2,1,0:T(8,128)(2,1)}), bf16[128,32,512]{2,1,0:T(8,128)(2,1)}, u32[]{:S(2)}, u32[]{:S(2)}) %all-to-all-start.1) | async-done | bytes 4194336 | tf_op jit(solution)/shard_map/all_to_all | solution.py:402
  144.4 6.0 %all-to-all-start = ((bf16[128,32,512]{2,1,0:T(8,128)(2,1)}), bf16[128,32,512]{2,1,0:T(8,128)(2,1)}, u32[]{:S(2)}, u32[]{:S(2)}) async-start(bf16[128,32,512]{2,1,0:T(8,128)(2,1)} %bitcast.50), calls=%async_computation | async-start | bytes 8388608 | tf_op jit(solution)/shard_map/all_to_all | solution.py:402
  159.3 16.5 %experts.2.rest_0_ = bf16[32,4,16,2048]{3,2,1,0:T(8,128)(2,1)} custom-call(bf16[32,4,32,512]{3,2,1,0:T(8,128)(2,1)} %bitcast.13.rows, f32[4,512]{1,0:T(4,128)} %reshape.97.gain, bf16[2048,1536]{1,0:T(8,128)(2,1)} %bitcast.56, bf16[768,2048]{1,0:T(8,128)(2,1)} %bitcast.58), custom_call_target="tpu_custom_call" | custom-call | flops 9663676416 | bytes 17825792 | tf_op jit(solution)/shard_map/experts/pallas_call | solution.py:292
  177.6 2.2 collective-permute-start.16
  179.8 1.6 collective-permute-start.17
  181.4 21.2 %all-to-all-done = bf16[128,32,512]{2,1,0:T(8,128)(2,1)} async-done(((bf16[128,32,512]{2,1,0:T(8,128)(2,1)}), bf16[128,32,512]{2,1,0:T(8,128)(2,1)}, u32[]{:S(2)}, u32[]{:S(2)}) %all-to-all-start) | async-done | bytes 4194336 | tf_op jit(solution)/shard_map/all_to_all | solution.py:402
  202.6 16.4 %experts.3 = bf16[32,4,16,2048]{3,2,1,0:T(8,128)(2,1)} custom-call(bf16[32,4,32,512]{3,2,1,0:T(8,128)(2,1)} %bitcast.8.rows, f32[4,512]{1,0:T(4,128)} %reshape.97.gain, bf16[2048,1536]{1,0:T(8,128)(2,1)} %bitcast.57, bf16[768,2048]{1,0:T(8,128)(2,1)} %bitcast.59, bf16[32,4,16,2048]{3,2,1,0:T(8,128)(2,1)} %experts.2.rest_0_), custom_call_target="tpu_custom_call", output_to_operand_aliasing={{}: (4, {})} | custom-call | flops 9663676416 | bytes 17825792 | tf_op jit(solution)/shard_map/experts/pallas_call | solution.py:292
  219.8 5.9 %all-to-all-start.2 = ((bf16[128,16,2048]{2,1,0:T(8,128)(2,1)}), bf16[128,16,2048]{2,1,0:T(8,128)(2,1)}, u32[]{:S(2)}, u32[]{:S(2)}) async-start(bf16[128,16,2048]{2,1,0:T(8,128)(2,1)} %bitcast.52), calls=%async_computation.2 | async-start | bytes 16777216 | tf_op jit(solution)/shard_map/all_to_all | solution.py:419
  226.1 1.9 join.1
  229.2 1.5 select_reduce_fusion
  230.7 103.0 %all-to-all-done.2 = bf16[128,16,2048]{2,1,0:T(8,128)(2,1)} async-done(((bf16[128,16,2048]{2,1,0:T(8,128)(2,1)}), bf16[128,16,2048]{2,1,0:T(8,128)(2,1)}, u32[]{:S(2)}, u32[]{:S(2)}) %all-to-all-start.2) | async-done | bytes 8388640 | tf_op jit(solution)/shard_map/all_to_all | solution.py:419
  333.8 5.7 %fusion = bf16[128,2048]{1,0:T(8,128)(2,1)} fusion(bf16[2048,2048]{1,0:T(8,128)(2,1)} %bitcast.24, bf16[128,2048]{1,0:T(8,128)(2,1)} %join.1, pred[128,2048]{1,0:T(32,128)(4,1)S(1)} %convolution_compare_fusion, s32[2048]{0:T(1024)S(1)} %get-tuple-element.84, pred[128,128]{0,1:T(32,128)(4,1)S(1)} %copy.26, f32[128,128]{0,1:T(8,128)S(1)} %get-tuple-element.81, ...), kind=kOutput, calls=%fused_computation.4 | convolution fusion | flops 1142505472 | bytes 9790464 | tf_op jit(solution)/shard_map/dot_general | solution.py:436
  (107 shorter events, 21.1 us)
Async XLA Ops:
  0.0 229.2 %copy-start = (bf16[2048,128]{1,0:T(8,128)(2,1)S(1)}, bf16[2048,128]{1,0:T(8,128)(2,1)}, u32[]{:S(2)}) copy-start(bf16[2048,128]{1,0:T(8,128)(2,1)} %param.29) | copy-start | bytes 1572868
  0.0 43.7 %copy-start.13 = (s32[1,512]{1,0:T(1,128)S(1)}, s32[1,512]{1,0:T(1,128)}, u32[]{:S(2)}) copy-start(s32[1,512]{1,0:T(1,128)} %refs_17_.1) | copy-start | bytes 6148
  0.0 43.9 %copy-start.29 = (f32[2048]{0:T(1024)S(1)}, f32[2048]{0:T(1024)}, u32[]{:S(2)}) copy-start(f32[2048]{0:T(1024)} %param.25) | copy-start | bytes 24580
  0.0 44.8 %copy-start.14 = (f32[128]{0:T(128)S(1)}, f32[128]{0:T(128)}, u32[]{:S(2)}) copy-start(f32[128]{0:T(128)} %param.26) | copy-start | bytes 1540
  0.0 44.8 %copy-start.15 = (f32[128]{0:T(128)S(1)}, f32[128]{0:T(128)}, u32[]{:S(2)}) copy-start(f32[128]{0:T(128)} %param.27) | copy-start | bytes 1540
  0.0 12.1 %collective-permute-start = (bf16[128,1280]{1,0:T(8,128)(2,1)}, bf16[128,1280]{1,0:T(8,128)(2,1)S(1)}, u32[]{:S(2)}, u32[]{:S(2)}) collective-permute-start(bf16[128,1280]{1,0:T(8,128)(2,1)} %own.1), channel_id=1, source_target_pairs={{0,1},{1,2},{2,3},{3,0},{4,5},{5,6},{6,7},{7,4},{8,9},{9,10},{10,1... | collective-permute-start | bytes 983048 | tf_op jit(solution)/shard_map/ppermute | solution.py:32
  2.1 16.5 %collective-permute-start.1 = (bf16[128,1280]{1,0:T(8,128)(2,1)}, bf16[128,1280]{1,0:T(8,128)(2,1)S(1)}, u32[]{:S(2)}, u32[]{:S(2)}) collective-permute-start(bf16[128,1280]{1,0:T(8,128)(2,1)} %own.1), channel_id=1, source_target_pairs={{0,3},{1,0},{2,1},{3,2},{4,7},{5,4},{6,5},{7,6},{8,11},{9,8},{10,9... | collective-permute-start | bytes 983048 | tf_op jit(solution)/shard_map/ppermute | solution.py:32
  4.3 16.0 %collective-permute-start.2 = (bf16[128,1280]{1,0:T(8,128)(2,1)}, bf16[128,1280]{1,0:T(8,128)(2,1)S(1)}, u32[]{:S(2)}, u32[]{:S(2)}) collective-permute-start(bf16[128,1280]{1,0:T(8,128)(2,1)} %own.1), channel_id=1, source_target_pairs={{0,2},{1,3},{2,0},{3,1},{4,6},{5,7},{6,4},{7,5},{8,10},{9,11},{10,... | collective-permute-start | bytes 983048 | tf_op jit(solution)/shard_map/ppermute | solution.py:32
  8.9 141.4 %copy-start.12 = (s32[4]{0:T(128)}, s32[4]{0:T(128)S(1)}, u32[]{:S(2)}) copy-start(s32[4]{0:T(128)S(1)} %compare_select_fusion.order.refs_0_) | copy-start | bytes 52
  25.4 18.6 %copy-start.1 = (bf16[288,512]{1,0:T(8,128)(2,1)}, bf16[288,512]{1,0:T(8,128)(2,1)S(1)}, u32[]{:S(2)}) copy-start(bf16[288,512]{1,0:T(8,128)(2,1)S(1)} %get-tuple-element.46.refs_1_.own) | copy-start | bytes 884740
  25.4 28.2 %copy-start.10 = (bf16[256,512]{1,0:T(8,128)(2,1)}, bf16[256,512]{1,0:T(8,128)(2,1)S(1)}, u32[]{:S(2)}) copy-start(bf16[256,512]{1,0:T(8,128)(2,1)S(1)} %get-tuple-element.39.refs_1_) | copy-start | bytes 786436
  25.4 14.9 %collective-permute-start.3 = (bf16[288,512]{1,0:T(8,128)(2,1)S(1)}, bf16[288,512]{1,0:T(8,128)(2,1)S(1)}, u32[]{:S(2)}, u32[]{:S(2)}) collective-permute-start(bf16[288,512]{1,0:T(8,128)(2,1)S(1)} %get-tuple-element.46.refs_1_.own), channel_id=1, source_target_pairs={{0,1},{1,2},{2,3},{3,0},{4,5},{5,6},{6,7},{7,4},{8,9},{9,10},{10,1... | collective-permute-start | bytes 884744 | tf_op jit(solution)/shard_map/ppermute | solution.py:32
  26.6 17.3 %collective-permute-start.4 = (bf16[288,512]{1,0:T(8,128)(2,1)S(1)}, bf16[288,512]{1,0:T(8,128)(2,1)S(1)}, u32[]{:S(2)}, u32[]{:S(2)}) collective-permute-start(bf16[288,512]{1,0:T(8,128)(2,1)S(1)} %get-tuple-element.46.refs_1_.own), channel_id=1, source_target_pairs={{0,3},{1,0},{2,1},{3,2},{4,7},{5,4},{6,5},{7,6},{8,11},{9,8},{10,9... | collective-permute-start | bytes 884744 | tf_op jit(solution)/shard_map/ppermute | solution.py:32
  28.7 15.2 %collective-permute-start.5 = (bf16[288,512]{1,0:T(8,128)(2,1)S(1)}, bf16[288,512]{1,0:T(8,128)(2,1)S(1)}, u32[]{:S(2)}, u32[]{:S(2)}) collective-permute-start(bf16[288,512]{1,0:T(8,128)(2,1)S(1)} %get-tuple-element.46.refs_1_.own), channel_id=1, source_target_pairs={{0,2},{1,3},{2,0},{3,1},{4,6},{5,7},{6,4},{7,5},{8,10},{9,11},{10,... | collective-permute-start | bytes 884744 | tf_op jit(solution)/shard_map/ppermute | solution.py:32
  40.3 16.6 %collective-permute-start.6 = (bf16[256,512]{1,0:T(8,128)(2,1)S(1)}, bf16[256,512]{1,0:T(8,128)(2,1)S(1)}, u32[]{:S(2)}, u32[]{:S(2)}) collective-permute-start(bf16[256,512]{1,0:T(8,128)(2,1)S(1)} %get-tuple-element.39.refs_1_), channel_id=1, source_target_pairs={{0,1},{1,2},{2,3},{3,0},{4,5},{5,6},{6,7},{7,4},{8,9},{9,10},{10,1... | collective-permute-start | bytes 786440 | tf_op jit(solution)/shard_map/ppermute | solution.py:32
  40.3 18.9 %collective-permute-start.7 = (bf16[256,512]{1,0:T(8,128)(2,1)S(1)}, bf16[256,512]{1,0:T(8,128)(2,1)S(1)}, u32[]{:S(2)}, u32[]{:S(2)}) collective-permute-start(bf16[256,512]{1,0:T(8,128)(2,1)S(1)} %get-tuple-element.39.refs_1_), channel_id=1, source_target_pairs={{0,3},{1,0},{2,1},{3,2},{4,7},{5,4},{6,5},{7,6},{8,11},{9,8},{10,9... | collective-permute-start | bytes 786440 | tf_op jit(solution)/shard_map/ppermute | solution.py:32
  43.5 15.7 %collective-permute-start.8 = (bf16[256,512]{1,0:T(8,128)(2,1)S(1)}, bf16[256,512]{1,0:T(8,128)(2,1)}, u32[]{:S(2)}, u32[]{:S(2)}) collective-permute-start(bf16[256,512]{1,0:T(8,128)(2,1)S(1)} %get-tuple-element.39.refs_1_), channel_id=1, source_target_pairs={{0,2},{1,3},{2,0},{3,1},{4,6},{5,7},{6,4},{7,5},{8,10},{9,11},{10,... | collective-permute-start | bytes 786440 | tf_op jit(solution)/shard_map/ppermute | solution.py:32
  53.6 20.4 %collective-permute-start.12 = (bf16[256,512]{1,0:T(8,128)(2,1)S(1)}, bf16[256,512]{1,0:T(8,128)(2,1)S(1)}, u32[]{:S(2)}, u32[]{:S(2)}) collective-permute-start(bf16[256,512]{1,0:T(8,128)(2,1)S(1)} %get-tuple-element.55), channel_id=1, source_target_pairs={{0,1},{1,2},{2,3},{3,0},{4,5},{5,6},{6,7},{7,4},{8,9},{9,10},{10,1... | collective-permute-start | bytes 786440 | tf_op jit(solution)/shard_map/ppermute | solution.py:32
  54.6 20.9 %collective-permute-start.13 = (bf16[256,512]{1,0:T(8,128)(2,1)S(1)}, bf16[256,512]{1,0:T(8,128)(2,1)S(1)}, u32[]{:S(2)}, u32[]{:S(2)}) collective-permute-start(bf16[256,512]{1,0:T(8,128)(2,1)S(1)} %get-tuple-element.56), channel_id=1, source_target_pairs={{0,3},{1,0},{2,1},{3,2},{4,7},{5,4},{6,5},{7,6},{8,11},{9,8},{10,9... | collective-permute-start | bytes 786440 | tf_op jit(solution)/shard_map/ppermute | solution.py:32
  56.9 18.5 %collective-permute-start.14 = (bf16[256,512]{1,0:T(8,128)(2,1)S(1)}, bf16[256,512]{1,0:T(8,128)(2,1)S(1)}, u32[]{:S(2)}, u32[]{:S(2)}) collective-permute-start(bf16[256,512]{1,0:T(8,128)(2,1)S(1)} %get-tuple-element.57), channel_id=1, source_target_pairs={{0,2},{1,3},{2,0},{3,1},{4,6},{5,7},{6,4},{7,5},{8,10},{9,11},{10,... | collective-permute-start | bytes 786440 | tf_op jit(solution)/shard_map/ppermute | solution.py:32
  60.0 12.6 %copy-start.7 = (bf16[288,512]{1,0:T(8,128)(2,1)S(1)}, bf16[288,512]{1,0:T(8,128)(2,1)}, u32[]{:S(2)}) copy-start(bf16[288,512]{1,0:T(8,128)(2,1)} %copy-done.6) | copy-start | bytes 884740
  60.0 12.6 %copy-start.9 = (bf16[288,512]{1,0:T(8,128)(2,1)S(1)}, bf16[288,512]{1,0:T(8,128)(2,1)}, u32[]{:S(2)}) copy-start(bf16[288,512]{1,0:T(8,128)(2,1)} %copy-done.8) | copy-start | bytes 884740
  71.0 7.8 %collective-permute-start.10 = (bf16[256,512]{1,0:T(8,128)(2,1)S(1)}, bf16[256,512]{1,0:T(8,128)(2,1)S(1)}, u32[]{:S(2)}, u32[]{:S(2)}) collective-permute-start(bf16[256,512]{1,0:T(8,128)(2,1)S(1)} %get-tuple-element.52), channel_id=1, source_target_pairs={{0,3},{1,0},{2,1},{3,2},{4,7},{5,4},{6,5},{7,6},{8,11},{9,8},{10,9... | collective-permute-start | bytes 786440 | tf_op jit(solution)/shard_map/ppermute | solution.py:32
  71.9 7.9 %collective-permute-start.11 = (bf16[256,512]{1,0:T(8,128)(2,1)S(1)}, bf16[256,512]{1,0:T(8,128)(2,1)S(1)}, u32[]{:S(2)}, u32[]{:S(2)}) collective-permute-start(bf16[256,512]{1,0:T(8,128)(2,1)S(1)} %get-tuple-element.53), channel_id=1, source_target_pairs={{0,2},{1,3},{2,0},{3,1},{4,6},{5,7},{6,4},{7,5},{8,10},{9,11},{10,... | collective-permute-start | bytes 786440 | tf_op jit(solution)/shard_map/ppermute | solution.py:32
  74.0 8.6 %collective-permute-start.9 = (bf16[256,512]{1,0:T(8,128)(2,1)S(1)}, bf16[256,512]{1,0:T(8,128)(2,1)S(1)}, u32[]{:S(2)}, u32[]{:S(2)}) collective-permute-start(bf16[256,512]{1,0:T(8,128)(2,1)S(1)} %get-tuple-element.51), channel_id=1, source_target_pairs={{0,1},{1,2},{2,3},{3,0},{4,5},{5,6},{6,7},{7,4},{8,9},{9,10},{10,1... | collective-permute-start | bytes 786440 | tf_op jit(solution)/shard_map/ppermute | solution.py:32
  83.3 61.1 %all-to-all-start.1 = ((bf16[128,32,512]{2,1,0:T(8,128)(2,1)}), bf16[128,32,512]{2,1,0:T(8,128)(2,1)}, u32[]{:S(2)}, u32[]{:S(2)}) async-start(bf16[128,32,512]{2,1,0:T(8,128)(2,1)} %bitcast.51), calls=%async_computation.1 | async-start | bytes 8388608 | tf_op jit(solution)/shard_map/all_to_all | solution.py:402
  144.4 58.2 %all-to-all-start = ((bf16[128,32,512]{2,1,0:T(8,128)(2,1)}), bf16[128,32,512]{2,1,0:T(8,128)(2,1)}, u32[]{:S(2)}, u32[]{:S(2)}) async-start(bf16[128,32,512]{2,1,0:T(8,128)(2,1)} %bitcast.50), calls=%async_computation | async-start | bytes 8388608 | tf_op jit(solution)/shard_map/all_to_all | solution.py:402
  159.3 16.5 %copy-start.17 = (bf16[256,512]{1,0:T(8,128)(2,1)S(1)}, bf16[256,512]{1,0:T(8,128)(2,1)}, u32[]{:S(2)}) copy-start(bf16[256,512]{1,0:T(8,128)(2,1)} %copy-done.16) | copy-start | bytes 786436
  176.6 42.4 %collective-permute-start.15 = (bf16[128,512]{1,0:T(8,128)(2,1)S(1)}, bf16[128,512]{1,0:T(8,128)(2,1)S(1)}, u32[]{:S(2)}, u32[]{:S(2)}) collective-permute-start(bf16[128,512]{1,0:T(8,128)(2,1)S(1)} %get-tuple-element.71), channel_id=1, source_target_pairs={{0,1},{1,2},{2,3},{3,0},{4,5},{5,6},{6,7},{7,4},{8,9},{9,10},{10,1... | collective-permute-start | bytes 393224 | tf_op jit(solution)/shard_map/ppermute | solution.py:32
  177.6 41.4 %collective-permute-start.16 = (bf16[128,512]{1,0:T(8,128)(2,1)S(1)}, bf16[128,512]{1,0:T(8,128)(2,1)S(1)}, u32[]{:S(2)}, u32[]{:S(2)}) collective-permute-start(bf16[128,512]{1,0:T(8,128)(2,1)S(1)} %get-tuple-element.70), channel_id=1, source_target_pairs={{0,3},{1,0},{2,1},{3,2},{4,7},{5,4},{6,5},{7,6},{8,11},{9,8},{10,9... | collective-permute-start | bytes 393224 | tf_op jit(solution)/shard_map/ppermute | solution.py:32
  179.8 39.2 %collective-permute-start.17 = (bf16[128,512]{1,0:T(8,128)(2,1)S(1)}, bf16[128,512]{1,0:T(8,128)(2,1)S(1)}, u32[]{:S(2)}, u32[]{:S(2)}) collective-permute-start(bf16[128,512]{1,0:T(8,128)(2,1)S(1)} %get-tuple-element.69), channel_id=1, source_target_pairs={{0,2},{1,3},{2,0},{3,1},{4,6},{5,7},{6,4},{7,5},{8,10},{9,11},{10,... | collective-permute-start | bytes 393224 | tf_op jit(solution)/shard_map/ppermute | solution.py:32
  219.8 114.0 %all-to-all-start.2 = ((bf16[128,16,2048]{2,1,0:T(8,128)(2,1)}), bf16[128,16,2048]{2,1,0:T(8,128)(2,1)}, u32[]{:S(2)}, u32[]{:S(2)}) async-start(bf16[128,16,2048]{2,1,0:T(8,128)(2,1)} %bitcast.52), calls=%async_computation.2 | async-start | bytes 16777216 | tf_op jit(solution)/shard_map/all_to_all | solution.py:419
  (20 other events, 76.1 us)
